TPU v7x, 256 devices: a whole 4x4x8 slice. The times are simulated.
256 devices in a mesh: row: 8 (over x, core), col: 8 (over z), depth: 4 (over y).
Axes of the slice: x: 4, y: 4, z: 8, core: 2. Of those that a mesh axis runs over, the one named last changes fastest.
Arguments:
- x_blocks: bfloat16 [8, 8, 4, 1, 2, 128, 128], P('row', 'col', 'depth'), may hold values from -6 to 6
- y_blocks: bfloat16 [8, 8, 4, 1, 4, 128, 128], P('row', 'col', 'depth'), may hold values from -0.03125 to 0.03125
- task_left: int32 [8, 8, 4, 8, 8, 16], P('row', 'col', 'depth'), may hold values from 0 to 1
- task_right: int32 [8, 8, 4, 8, 8, 16], P('row', 'col', 'depth'), may hold values from 0 to 3
- colloc_block: int32 [8, 8, 4, 64, 1], P('row', 'col', 'depth'), may hold values from 0 to 3
- live: int32 [8, 8, 4, 64], P('row', 'col', 'depth'), may hold values from 0 to 1
- factors: bfloat16 [8, 8, 4, 64, 1, 2, 3, 8, 128], P('row', 'col', 'depth'), may hold values from 0.099609375 to 1
- cube_anchor: int32 [8, 8, 4, 64, 1, 3], P('row', 'col', 'depth'), may hold values from 0 to 256, as said below
Outputs:
- density: bfloat16 [8, 8, 16, 128, 128], P('row', 'col', 'depth')
- charge: float32 [64, 2048, 2048], P('depth', 'row', 'col')
Inputs may be any that keep to these rules, and one draw needn't show every extreme that they name: `cube_anchor`: component 0 of each corner is at most 16; components 1 and 2 are at most 256.
All inputs are finite; a program needn't handle non-finite values.
Results may differ from a plain program's by a relative error of at most 0.0059.
Values may be sent and summed in bfloat16 or wider, within the bound.
A program may use at most 128 MiB of HBM per device.

v0:
```python
import functools

import jax
import jax.numpy as jnp
from jax import lax
from jax.experimental import pallas as pl
from jax.experimental.pallas import tpu as pltpu
from jax.sharding import PartitionSpec as P

BLK = 128
NA = 2
NB = 4
NC = 16
CUBE = 8
HALO = 4
BZ = 16
BXY = 256
CELLS = CUBE * CUBE * CUBE
SCALE = 0.0625
F32 = jnp.float32
BF16 = jnp.bfloat16
MESH = pl.DeviceIdType.MESH
NT = (((1,), (1,)), ((), ()))


def product_kernel(
    x_ref, y_ref, left_ref, right_ref, block_ref, live_ref, factor_ref, anchor_ref,
    density_ref, own_ref, below_ref, above_ref, near_anchor_ref,
    xg, yg, kmat, rhs, total, part_out, part_in, b0, b1, pairs, cubes, first_in, second_out,
    own_in, below_in, above_in,
    xr_send, xr_recv, xl_send, xl_recv, yr_send, yr_recv, yl_send, yl_recv, ys_send, ys_recv,
    part_send, part_recv, first_send, first_recv, second_send, second_recv, anchor_send, anchor_recv,
):
    nr, nc, nd = lax.axis_size("row"), lax.axis_size("col"), lax.axis_size("depth")
    chips = nr // 2
    r, c, d = lax.axis_index("row"), lax.axis_index("col"), lax.axis_index("depth")
    core = lax.rem(r, 2)
    chip = r // 2
    sibling = r + 1 - 2 * core

    def up(i, j, n):
        return lax.rem(i + j, n)

    def send(src, dst, s, t, row, col, depth):
        copy = pltpu.make_async_remote_copy(
            src_ref=src, dst_ref=dst, send_sem=s, recv_sem=t, device_id=(row, col, depth), device_id_type=MESH
        )
        copy.start()
        return copy

    barrier = pltpu.get_barrier_semaphore()
    greeted = 0
    for j in range(1, nr):
        pl.semaphore_signal(barrier, inc=1, device_id=(up(r, j, nr), c, d), device_id_type=MESH)
        greeted += 1
    for j in range(nc):
        for k in (0, 1, nd - 1):
            if j or k:
                pl.semaphore_signal(barrier, inc=1, device_id=(r, up(c, j, nc), up(d, k, nd)), device_id_type=MESH)
                greeted += 1
    for k in range(2, nd - 1):
        pl.semaphore_signal(barrier, inc=1, device_id=(r, c, up(d, k, nd)), device_id_type=MESH)
        greeted += 1
    pl.semaphore_wait(barrier, greeted)

    copies = []
    right, left = up(c, 1, nc), up(c, nc - 1, nc)
    chip_r, chip_l = up(chip, 1, chips) * 2 + core, up(chip, chips - 1, chips) * 2 + core
    half = nc // 2

    def x_step(h):
        rows_r = pl.ds(0, 256) if h < half else pl.ds(0, 128)
        rows_l = pl.ds(0, 256) if h < half else pl.ds(128, 128)
        src_r, src_l = up(c, nc - (h - 1), nc), up(c, h - 1, nc)
        copies.append(
            send((x_ref if h == 1 else xg.at[src_r]).at[rows_r], xg.at[src_r, rows_r], xr_send.at[h - 1], xr_recv.at[h - 1], r, right, d)
        )
        copies.append(
            send((x_ref if h == 1 else xg.at[src_l]).at[rows_l], xg.at[src_l, rows_l], xl_send.at[h - 1], xl_recv.at[h - 1], r, left, d)
        )

    def x_wait(h):
        rows_r = pl.ds(0, 256) if h < half else pl.ds(0, 128)
        rows_l = pl.ds(0, 256) if h < half else pl.ds(128, 128)
        src_r, src_l = up(c, nc - h, nc), up(c, h, nc)
        pltpu.make_async_copy(xg.at[src_r, rows_r], xg.at[src_r, rows_r], xr_recv.at[h - 1]).wait()
        pltpu.make_async_copy(xg.at[src_l, rows_l], xg.at[src_l, rows_l], xl_recv.at[h - 1]).wait()

    def y_wait(slot, rows, sem):
        pltpu.make_async_copy(yg.at[slot, rows], yg.at[slot, rows], sem).wait()

    def y_share(q):
        slot = up(r, 2 * q, nr)
        copies.append(send(y_ref if q == 0 else yg.at[slot], yg.at[slot], ys_send.at[q], ys_recv.at[q], sibling, c, d))

    whole, lower, upper = pl.ds(0, 512), pl.ds(0, 256), pl.ds(256, 256)
    x_step(1)
    y_share(0)
    copies.append(send(y_ref, yg.at[r], yr_send.at[0], yr_recv.at[0], chip_r, c, d))
    copies.append(send(y_ref, yg.at[r], yl_send.at[0], yl_recv.at[0], chip_l, c, d))
    for i, k in enumerate((1, nd - 1)):
        copies.append(send(anchor_ref, near_anchor_ref.at[i], anchor_send.at[i], anchor_recv.at[i], r, c, up(d, k, nd)))

    npair = NA * NB
    task = left_ref[...] * NB + right_ref[...]
    counts = jnp.concatenate(
        [jnp.sum(jnp.where(task == p, 1.0, 0.0).astype(F32), axis=1) for p in range(npair)], axis=0
    )
    pick_out = (lax.broadcasted_iota(jnp.int32, (256, NC), 0) // 16 == lax.broadcasted_iota(jnp.int32, (256, NC), 1))
    spread = lax.dot_general(pick_out.astype(F32), counts, NT, preferred_element_type=F32)
    npanel = left_ref.shape[0]
    row64 = lax.broadcasted_iota(jnp.int32, (npair * npanel, npair * 16), 0)
    lane64 = lax.broadcasted_iota(jnp.int32, (npair * npanel, npair * 16), 1)
    same = lax.rem(lax.broadcasted_iota(jnp.int32, (256, 128), 0), 16) == lax.rem(
        lax.broadcasted_iota(jnp.int32, (256, 128), 1), 16
    )
    for k in range(npanel):
        pick_in = (row64 == (lane64 // 16) * npanel + k).astype(BF16)
        m = jnp.dot(spread.astype(BF16), pick_in, preferred_element_type=F32)
        m = jnp.where(same, m, 0.0).astype(BF16)
        kmat[k, :, 0:128] = m
        kmat[k, :, 128:256] = m

    pairs[...] = jnp.zeros_like(pairs)

    def basis(lo, hi):
        @pl.loop(lo, hi)
        def _(t):
            for w in range(2):
                k = t * 2 + w
                f = factor_ref[pl.ds(pl.multiple_of(k * 48, 16), 48), :].astype(F32)
                for e, out in ((0, b0), (1, b1)):
                    f0, f1, f2 = (f[24 * e + 8 * i : 24 * e + 8 * i + 8] for i in range(3))
                    for a in range(CUBE):
                        g = f0[a : a + 1] * f1
                        for b in range(0, CUBE, 2):
                            two = jnp.concatenate([g[b : b + 1] * f2, g[b + 1 : b + 2] * f2], axis=0)
                            out[t, a * 64 + b * 8 : a * 64 + b * 8 + 16, w * 128 : w * 128 + 128] = two.astype(BF16)

    def stage_panel(delta):
        for b in range(NB):
            xs = x_ref if delta == 0 else xg.at[up(c, delta, nc)]
            ys = y_ref if delta == 0 else yg.at[up(r, delta, nr)]
            p = jnp.dot(xs[...], ys[b * 128 : b * 128 + 128, :], preferred_element_type=F32)
            high = p.astype(BF16)
            low = (p - high.astype(F32)).astype(BF16)
            for a in range(NA):
                at = (a * NB + b) * 16
                for ch in range(8):
                    rows = slice(a * 128 + ch * 16, a * 128 + ch * 16 + 16)
                    rhs[at : at + 16, ch * 128 : ch * 128 + 128] = high[rows]
                    rhs[128 + at : 128 + at + 16, ch * 128 : ch * 128 + 128] = low[rows]

    def panel(delta):
        stage_panel(delta)
        k = lax.rem(r + c + delta, npanel)
        got = jnp.dot(kmat[k], rhs[...], preferred_element_type=F32)
        if delta == 0:
            total[...] = got
        else:
            total[...] += got

    nslot = factor_ref.shape[0] // 48
    quarter = nslot // 8

    panel(0)
    x_wait(1)
    x_step(2)
    y_wait(up(r, nr - 2, nr), whole, yr_recv.at[0])
    copies.append(
        send(yg.at[up(r, nr - 2, nr), lower], yg.at[up(r, nr - 2, nr), lower], yr_send.at[1], yr_recv.at[1], chip_r, c, d)
    )
    y_wait(up(r, 2, nr), whole, yl_recv.at[0])
    copies.append(send(yg.at[up(r, 2, nr), upper], yg.at[up(r, 2, nr), upper], yl_send.at[1], yl_recv.at[1], chip_l, c, d))
    y_share(chips - 1)
    y_share(1)
    basis(0, quarter)
    x_wait(2)
    x_step(3)
    y_wait(up(r, 4, nr), lower, yr_recv.at[1])
    y_wait(up(r, 4, nr), upper, yl_recv.at[1])
    y_share(2)
    panel(2)
    panel(nr - 2)
    basis(quarter, 2 * quarter)
    x_wait(3)
    x_step(4)
    for q in range(chips):
        y_wait(lax.rem(sibling + 2 * q, nr), whole, ys_recv.at[q])
    for delta in (1, nr - 1, 3, nr - 3):
        panel(delta)
    basis(2 * quarter, 3 * quarter)
    x_wait(4)
    stage_panel(half)
    k = lax.rem(r + c + half, npanel)

    def last(dest):
        rows = pl.ds(pl.multiple_of(dest * 64, 64), 64)
        return total[rows, :] + jnp.dot(kmat[k, rows, :], rhs[...], preferred_element_type=F32)

    for j in (2, 1, 3):
        dest = up(d, j, nd)
        part_out[j - 1] = last(dest).astype(BF16)
        copies.append(send(part_out.at[j - 1], part_in.at[j - 1], part_send.at[j - 1], part_recv.at[j - 1], r, c, dest))
    summed = last(d)
    basis(3 * quarter, 4 * quarter)
    for j in (1, 3, 2):
        pltpu.make_async_copy(part_in.at[j - 1], part_in.at[j - 1], part_recv.at[j - 1]).wait()
        summed = summed + part_in[j - 1].astype(F32)
    density = summed.astype(BF16)
    for o in range(NC // 4):
        for ch in range(8):
            density_ref[o, ch * 16 : ch * 16 + 16, :] = density[o * 16 : o * 16 + 16, ch * 128 : ch * 128 + 128]
    for i in range(4):
        for j in range(4):
            pairs[i * 4 + j, 0:128, 0:128] = density_ref[i]
            pairs[i * 4 + j, 128:256, 128:256] = density_ref[j]

    row16 = lax.broadcasted_iota(jnp.int32, (16, 256), 0)
    side = lax.broadcasted_iota(jnp.int32, (16, 256), 1) // 128
    for j in (2, 1, 3, 0):
        group = up(chip, j, chips)
        base = group * 8

        def two(i, acc):
            t = base + i
            which = block_ref[t * 2] * 4 + block_ref[t * 2 + 1]
            ones = jnp.where(
                row16 == i * 2 + side,
                jnp.where(side == 0, jnp.minimum(live_ref[t * 2], 1), jnp.minimum(live_ref[t * 2 + 1], 1)).astype(F32) * SCALE,
                0.0,
            ).astype(BF16)
            weight = pairs[which]
            new = []
            for q in range(4):
                rows = pl.ds(q * 128, 128)
                v = jnp.dot(b0[t, rows, :], weight, preferred_element_type=F32)
                v = (v * b1[t, rows, :].astype(F32)).astype(BF16)
                new.append(acc[q] + lax.dot_general(ones, v, NT, preferred_element_type=F32))
            return tuple(new)

        acc = lax.fori_loop(0, 8, two, tuple(jnp.zeros((16, 128), F32) for _ in range(4)))
        for q in range(4):
            cubes[j, q] = acc[q]
        for w in range(2):
            owner = group * 2 + w
            if j:
                copies.append(
                    send(cubes.at[j, :, pl.ds(8 * w, 8)], first_in.at[:, pl.ds(pl.multiple_of(r * 8, 8), 8)], first_send.at[2 * j + w], first_recv.at[r], owner, c, d)
                )
    mine = pl.ds(pl.multiple_of(core * 8, 8), 8)
    theirs = pl.ds(pl.multiple_of(8 - core * 8, 8), 8)
    here = pl.ds(pl.multiple_of(r * 8, 8), 8)
    copies.append(send(cubes.at[0, :, theirs], first_in.at[:, here], first_send.at[0], first_recv.at[r], sibling, c, d))
    first_in[:, here, :] = cubes[0, :, mine, :]
    for j in range(1, nr):
        src = up(r, j, nr)
        rows = first_in.at[:, pl.ds(pl.multiple_of(src * 8, 8), 8)]
        pltpu.make_async_copy(rows, rows, first_recv.at[src]).wait()

    for s in range(nc):
        got = [first_in[q, pl.ds(s, 8, stride=8), :] for q in range(4)]
        for h in range(2):
            second_out[s, h] = jnp.concatenate(got[2 * h : 2 * h + 2], axis=0).astype(BF16)
    for j in [*range(1, nc), 0]:
        s = up(c, j, nc)
        copies.append(send(second_out.at[s, 1], below_in.at[c], second_send.at[1, j], second_recv.at[1, c], r, s, up(d, 1, nd)))
        copies.append(send(second_out.at[s, 0], above_in.at[c], second_send.at[2, j], second_recv.at[2, c], r, s, up(d, nd - 1, nd)))
        if j:
            copies.append(send(second_out.at[s], own_in.at[c], second_send.at[0, j], second_recv.at[0, c], r, s, d))
    own_ref[c] = second_out[c]
    for j in range(nc):
        s = up(c, j, nc)
        if j:
            pltpu.make_async_copy(own_in.at[s], own_in.at[s], second_recv.at[0, s]).wait()
            own_ref[s] = own_in[s]
        pltpu.make_async_copy(below_in.at[s], below_in.at[s], second_recv.at[1, s]).wait()
        below_ref[s] = below_in[s]
        pltpu.make_async_copy(above_in.at[s], above_in.at[s], second_recv.at[2, s]).wait()
        above_ref[s] = above_in[s]
    for i in range(2):
        pltpu.make_async_copy(near_anchor_ref.at[i], near_anchor_ref.at[i], anchor_recv.at[i]).wait()
    for copy in copies:
        copy.wait_send()


def product(x, y, left, right, block, live, factor, anchor, nr, nc):
    vmem = pl.BlockSpec(memory_space=pltpu.VMEM)
    smem = pl.BlockSpec(memory_space=pltpu.SMEM)
    hbm = pl.BlockSpec(memory_space=pl.ANY)
    dma = pltpu.SemaphoreType.DMA
    slots = block.shape[0]
    return pl.pallas_call(
        product_kernel,
        out_shape=(
            jax.ShapeDtypeStruct((NC // 4, BLK, BLK), BF16),
            jax.ShapeDtypeStruct((nc, 2, 16, 128), BF16),
            jax.ShapeDtypeStruct((nc, 16, 128), BF16),
            jax.ShapeDtypeStruct((nc, 16, 128), BF16),
            jax.ShapeDtypeStruct((2, *anchor.shape), jnp.int32),
        ),
        in_specs=[vmem, vmem, vmem, vmem, smem, smem, vmem, hbm],
        out_specs=(vmem, vmem, vmem, vmem, hbm),
        scratch_shapes=[
            pltpu.VMEM((nc, 256, 128), BF16),
            pltpu.VMEM((nr, 512, 128), BF16),
            pltpu.VMEM((8, 256, 256), BF16),
            pltpu.VMEM((256, 1024), BF16),
            pltpu.VMEM((256, 1024), F32),
            pltpu.VMEM((3, 64, 1024), BF16),
            pltpu.VMEM((3, 64, 1024), BF16),
            pltpu.VMEM((slots // 2, CELLS, 256), BF16),
            pltpu.VMEM((slots // 2, CELLS, 256), BF16),
            pltpu.VMEM((16, 256, 256), BF16),
            pltpu.VMEM((4, 4, 16, 128), F32),
            pltpu.VMEM((4, nr * 8, 128), F32),
            pltpu.VMEM((nc, 2, 16, 128), BF16),
            pltpu.VMEM((nc, 2, 16, 128), BF16),
            pltpu.VMEM((nc, 16, 128), BF16),
            pltpu.VMEM((nc, 16, 128), BF16),
            dma((4,)), dma((4,)), dma((4,)), dma((4,)),
            dma((2,)), dma((2,)), dma((2,)), dma((2,)), dma((4,)), dma((4,)),
            dma((3,)), dma((3,)), dma((8,)), dma((8,)), dma((3, 8)), dma((3, 8)), dma((2,)), dma((2,)),
        ],
        compiler_params=pltpu.CompilerParams(collective_id=0, has_side_effects=True, vmem_limit_bytes=56 * 1024 * 1024),
        name="product_and_cubes",
    )(x, y, left, right, block, live, factor, anchor)


def extended(x, sides, width):
    for axis, dim in sides:
        peers, length = (lax.axis_size(axis), x.shape[dim])
        up = [(i, (i + 1) % peers) for i in range(peers)]
        down = [(j, i) for i, j in up]
        last = lax.slice_in_dim(x, length - width, length, axis=dim)
        first = lax.slice_in_dim(x, 0, width, axis=dim)
        before = lax.ppermute(last, axis, up)
        after = lax.ppermute(first, axis, down)
        x = jnp.concatenate([before, x, after], axis=dim)
    return x


def fold_rims(grown_brick, along_dim, inner_len, rim_width):
    extent = grown_brick.shape[along_dim]
    centre = lax.slice_in_dim(grown_brick, 2 * rim_width, 2 * rim_width + inner_len, axis=along_dim)
    lower_rim = lax.slice_in_dim(grown_brick, 0, rim_width, axis=along_dim)
    upper_rim = lax.slice_in_dim(grown_brick, extent - rim_width, extent, axis=along_dim)
    pad_shape = list(lower_rim.shape)
    pad_shape[along_dim] = inner_len - rim_width
    filler = jnp.zeros(tuple(pad_shape), jnp.float32)
    return (
        centre
        + jnp.concatenate([lower_rim, filler], axis=along_dim)
        + jnp.concatenate([filler, upper_rim], axis=along_dim)
    )


def place_cubes(cube_values, corner, nz, nxy):
    offsets = jnp.arange(CUBE, dtype=jnp.int32)
    z_cells = jnp.arange(nz, dtype=jnp.int32)
    xy_cells = jnp.arange(nxy, dtype=jnp.int32)
    pick_z, pick_x, pick_y = (
        (cells[None, :, None] == corner[:, i][:, None, None] + offsets[None, None, :]).astype(jnp.float32)
        for i, cells in enumerate((z_cells, xy_cells, xy_cells))
    )
    along_y = jnp.einsum("kabt,kyt->kaby", cube_values, pick_y, precision=lax.Precision.HIGHEST)
    along_z = jnp.einsum("kza,kaby->zkby", pick_z, along_y, precision=lax.Precision.HIGHEST)
    return jnp.einsum("zkby,kxb->zxy", along_z, pick_x, precision=lax.Precision.HIGHEST)


def local(x_blocks, y_blocks, task_left, task_right, colloc_block, live, factors, cube_anchor):
    nr, nc = lax.axis_size("row"), lax.axis_size("col")
    density, own, below, above, near = product(
        x_blocks.reshape(NA * BLK, BLK),
        y_blocks.reshape(NB * BLK, BLK),
        task_left[0, 0, 0],
        task_right[0, 0, 0],
        colloc_block.reshape(-1),
        live.reshape(-1),
        factors.reshape(-1, BLK),
        cube_anchor[0, 0, 0],
        nr, nc,
    )
    zero = jnp.zeros((64, 256), F32)
    own = own.astype(F32).reshape(nc, 2, 2, 8, 128).transpose(3, 0, 1, 2, 4).reshape(64, 512)
    below = below.astype(F32).reshape(nc, 2, 8, 128).transpose(2, 0, 1, 3).reshape(64, 256)
    above = above.astype(F32).reshape(nc, 2, 8, 128).transpose(2, 0, 1, 3).reshape(64, 256)
    values = jnp.concatenate([own, jnp.concatenate([zero, below], 1), jnp.concatenate([above, zero], 1)], 0)
    corner = jnp.concatenate([cube_anchor.reshape(-1, 3), near[0].reshape(-1, 3), near[1].reshape(-1, 3)], 0)
    shift = jnp.concatenate([jnp.full((64,), -4), jnp.full((64,), -20), jnp.full((64,), 12)]).astype(jnp.int32)
    corner = corner.at[:, 0].add(shift)
    brick = place_cubes(values.reshape(-1, CUBE, CUBE, CUBE), corner, BZ, BXY + 2 * HALO)
    grown_brick = extended(brick, (("row", 1), ("col", 2)), HALO)
    charge = fold_rims(grown_brick, 1, BXY, HALO)
    charge = fold_rims(charge, 2, BXY, HALO)
    return (density[None, None], charge)


def solution(mesh):
    placed = tuple(P("row", "col", "depth", *(None,) * n) for n in (4, 4, 3, 3, 2, 1, 6, 3))
    return jax.shard_map(
        local,
        mesh=mesh,
        in_specs=placed,
        out_specs=(P("row", "col", "depth", None, None), P("depth", "row", "col")),
        check_vma=False,
    )
```

profile of v0, /device:TPU:1, one launch (start us, length us, event | category | flops | bytes accessed | tf_op | source)
XLA Modules:
  0.0 191.3 jit_solution(2010351924353431693)
XLA Ops:
  0.6 1.4 copy.39
  2.0 0.7 copy.76
  2.7 0.6 compare_reduce_fusion
  3.3 54.9 %product_and_cubes.1 = (bf16[4,128,128]{2,1,0:T(8,128)(2,1)}, bf16[8,2,16,128]{3,2,1,0:T(8,128)(2,1)}, bf16[8,16,128]{2,1,0:T(8,128)(2,1)}, bf16[8,16,128]{2,1,0:T(8,128)(2,1)}, s32[2,64,1,3]{3,2,1,0:T(1,128)}) custom-call(bf16[256,128]{1,0:T(8,128)(2,1)} %bitcast.69, bf16[512,128]{1,0:T(8,128)(2,1)} %bitcast.62, s32[8,8,16]{2,1,0:T(8,128)} %bitcast.71, ...), custom_call_target="tpu_custom_call" | custom-call | tf_op jit(solution)/shard_map/product_and_cubes/pallas_call | solution.py:293
  58.3 0.8 copy.74
  59.1 0.1 copy.62
  59.2 1.6 copy.48
  60.8 0.8 copy.75
  61.6 0.1 copy.61
  61.7 1.6 copy.47
  63.3 0.9 copy.73
  64.2 1.2 concatenate.43
  65.4 0.8 fusion.26
  66.2 0.1 copy.41
  66.2 0.1 copy.40
  66.3 1.4 pad_add_fusion.3
  67.7 0.1 iota_add_fusion.1
  67.8 0.1 iota_add_fusion
  67.9 0.7 pad_maximum_fusion.1
  68.7 7.8 %fusion.11 = f32[192,8,8,264]{3,1,2,0:T(8,128)} fusion(bf16[192,8,8,8]{3,2,1,0:T(8,128)(2,1)S(1)} %pad_maximum_fusion.1, s32[192,8]{1,0:T(8,128)S(1)} %iota_add_fusion.1), kind=kOutput, calls=%fused_computation.19 | convolution fusion | flops 52310016 | bytes 13178880 | tf_op jit(solution)/shard_map/kabt,kyt->kaby/dot_general | solution.py:366
  76.5 28.5 %convolution_bitcast_fusion = f32[16,192,8,264]{3,0,2,1:T(8,128)} fusion(f32[192,8,8,264]{3,1,2,0:T(8,128)} %fusion.11, s32[192,8]{1,0:T(8,128)S(1)} %iota_add_fusion), kind=kOutput, calls=%fused_computation.2 | convolution fusion | flops 622878720 | bytes 38934528 | tf_op jit(solution)/shard_map/kza,kaby->zkby/dot_general | solution.py:367
  104.9 48.0 %fusion.13 = f32[16,264,264]{2,1,0:T(8,128)S(1)} fusion(f32[16,192,8,264]{3,0,2,1:T(8,128)} %convolution_bitcast_fusion, s32[192,8]{0,1:T(8,128)S(1)} %iota_add_fusion.2), kind=kOutput, calls=%fused_computation.21 | convolution fusion | flops 20554592256 | bytes 30418944 | tf_op jit(solution)/shard_map/zkby,kxb->zxy/dot_general | solution.py:368
  153.0 0.0 copy-start
  153.1 0.2 collective-permute-start.1
  153.2 1.6 collective-permute-start
  154.8 2.3 %collective-permute-done.1 = f32[16,4,264]{2,1,0:T(4,128)S(1)} collective-permute-done((f32[16,4,264]{2,1,0:T(4,128)S(1)}, f32[16,4,264]{2,1,0:T(4,128)S(1)}, u32[]{:S(2)}, u32[]{:S(2)}) %collective-permute-start.1) | collective-permute-done | bytes 67616 | tf_op jit(solution)/shard_map/ppermute | solution.py:338
  157.1 0.0 collective-permute-done
  157.1 0.0 copy-done
  157.1 2.1 %pad_maximum_fusion.4 = (f32[16,272,4]{2,1,0:T(8,128)S(1)}, f32[16,272,4]{2,1,0:T(8,128)}) fusion(f32[16,4,264]{2,1,0:T(4,128)S(1)} %collective-permute-done.1, f32[16,264,264]{2,1,0:T(8,128)S(1)} %fusion.13, f32[16,4,264]{2,1,0:T(4,128)S(1)} %collective-permute-done), kind=kLoop, calls=%fused_computation.26 | loop fusion | flops 69632 | bytes 4734976 | tf_op jit(solution)/shard_map/slice | solution.py:335
  159.2 2.5 %copy.52 = f32[16,272,4]{1,0,2:T(8,128)S(1)} copy(f32[16,272,4]{2,1,0:T(8,128)} %get-tuple-element.25) | data formatting | bytes 139264 | tf_op jit(solution)/shard_map/slice | solution.py:336
  161.8 1.8 collective-permute-start.3
  163.6 0.9 copy.51
  164.5 0.1 collective-permute-start.2
  164.6 0.7 collective-permute-done.3
  165.3 2.1 %copy.54 = f32[16,272,4]{2,1,0:T(8,128)} copy(f32[16,272,4]{1,0,2:T(8,128)S(1)} %collective-permute-done.3) | data formatting | bytes 139264 | tf_op jit(solution)/shard_map/ppermute | solution.py:338
  167.4 1.9 collective-permute-done.2
  169.3 0.0 slice-start
  169.3 2.2 %copy.53 = f32[16,272,4]{2,1,0:T(8,128)} copy(f32[16,272,4]{1,0,2:T(8,128)S(1)} %collective-permute-done.2) | data formatting | bytes 139264 | tf_op jit(solution)/shard_map/ppermute | solution.py:337
  171.4 0.0 copy-start.2
  171.4 7.1 %pad_maximum_fusion = f32[16,272,272]{2,1,0:T(8,128)S(1)} fusion(f32[16,272,4]{2,1,0:T(8,128)} %copy.54, f32[16,4,264]{2,1,0:T(4,128)S(1)} %collective-permute-done.1, f32[16,264,264]{2,1,0:T(8,128)} %copy-done, f32[16,4,264]{2,1,0:T(4,128)S(1)} %collective-permute-done, f32[16,272,4]{2,1,0:T(8,128)} %copy.53), kind=kLoop, calls=%fused_computation.3 | loop fusion | flops 4734976 | bytes 9469952 | tf_op jit(solution)/shard_map/concatenate | solution.py:339
  178.6 0.0 slice-done
  178.6 0.0 slice-done.1
  178.6 0.0 copy-done.2
  178.6 7.7 %fusion.2 = f32[16,256,272]{2,1,0:T(8,128)S(1)} fusion(f32[16,272,4]{2,1,0:T(8,128)} %copy.54, f32[16,272,4]{2,1,0:T(8,128)} %copy.53, f32[16,4,264]{2,1,0:T(4,128)S(1)} %collective-permute-done.1, f32[16,264,264]{2,1,0:T(8,128)S(1)} %bitcast.57, f32[16,4,264]{2,1,0:T(4,128)S(1)} %collective-permute-done, f32[16,272,272]{2,1,0:T(8,128)S(1)} %pad_maximum_fusion, ...), kind=kLoop, calls=%fused_computation.5 | loop fusion | flops 14483456 | bytes 18104576 | tf_op jit(solution)/shard_map/add | solution.py:352
  186.3 0.6 slice.86
  186.9 3.7 %fusion.10 = f32[16,256,256]{2,1,0:T(8,128)} fusion(f32[16,256,272]{2,1,0:T(8,128)S(1)} %fusion.2, f32[16,256,4]{2,1,0:T(8,128)S(1)} %slice.86, pred[256]{0:T(512)(128)(4,1)S(1)} %copy-done.2), kind=kLoop, calls=%fused_computation.17 | loop fusion | flops 3145728 | bytes 12648704 | tf_op jit(solution)/shard_map/add | solution.py:352
  190.6 0.0 copy-done.1
  190.6 0.7 copy.78
  (7 shorter events, 0.1 us)
Async XLA Ops:
  153.0 4.1 %copy-start = (f32[16,264,264]{2,1,0:T(8,128)}, f32[16,264,264]{2,1,0:T(8,128)S(1)}, u32[]{:S(2)}) copy-start(f32[16,264,264]{2,1,0:T(8,128)S(1)} %fusion.13) | copy-start | bytes 13381636
  153.1 4.1 %collective-permute-start.1 = (f32[16,4,264]{2,1,0:T(4,128)S(1)}, f32[16,4,264]{2,1,0:T(4,128)S(1)}, u32[]{:S(2)}, u32[]{:S(2)}) collective-permute-start(f32[16,4,264]{2,1,0:T(4,128)S(1)} %get-tuple-element.27), channel_id=1, source_target_pairs={{32,0},{64,32},{96,64},{128,96},{160,128},{192,160},{224,192},{0,2... | collective-permute-start | bytes 202760 | tf_op jit(solution)/shard_map/ppermute | solution.py:338
  153.2 3.9 %collective-permute-start = (f32[16,4,264]{2,1,0:T(4,128)S(1)}, f32[16,4,264]{2,1,0:T(4,128)S(1)}, u32[]{:S(2)}, u32[]{:S(2)}) collective-permute-start(f32[16,4,264]{2,1,0:T(4,128)S(1)} %get-tuple-element.26), channel_id=1, source_target_pairs={{0,32},{32,64},{64,96},{96,128},{128,160},{160,192},{192,224},{224... | collective-permute-start | bytes 202760 | tf_op jit(solution)/shard_map/ppermute | solution.py:337
  161.8 3.5 %collective-permute-start.3 = (f32[16,272,4]{1,0,2:T(8,128)S(1)}, f32[16,272,4]{1,0,2:T(8,128)S(1)}, u32[]{:S(2)}, u32[]{:S(2)}) collective-permute-start(f32[16,272,4]{1,0,2:T(8,128)S(1)} %copy.52), channel_id=1, source_target_pairs={{4,0},{8,4},{12,8},{16,12},{20,16},{24,20},{28,24},{0,28},{5,1},{9... | collective-permute-start | bytes 208904 | tf_op jit(solution)/shard_map/ppermute | solution.py:338
  164.5 4.7 %collective-permute-start.2 = (f32[16,272,4]{1,0,2:T(8,128)S(1)}, f32[16,272,4]{1,0,2:T(8,128)S(1)}, u32[]{:S(2)}, u32[]{:S(2)}) collective-permute-start(f32[16,272,4]{1,0,2:T(8,128)S(1)} %copy.51), channel_id=1, source_target_pairs={{0,4},{4,8},{8,12},{12,16},{16,20},{20,24},{24,28},{28,0},{1,5},{5... | collective-permute-start | bytes 208904 | tf_op jit(solution)/shard_map/ppermute | solution.py:337
  169.3 9.3 %slice-start = ((s8[6488064]{0:T(1024)(128)(4,1)}), s8[2293760]{0:T(1024)(128)(4,1)S(1)}, s32[]{:S(2)}) async-start(s8[6488064]{0:T(1024)(128)(4,1)} %bitcast.56), calls=%async_computation | async-start | bytes 4587520
  171.4 7.2 %slice-start.1 = ((s8[6488064]{0:T(1024)(128)(4,1)}), s8[4194304]{0:T(1024)(128)(4,1)S(1)}, s32[]{:S(2)}) async-start(s8[6488064]{0:T(1024)(128)(4,1)} %bitcast.56), calls=%async_computation.1 | async-start | bytes 8388608
  171.4 7.2 %copy-start.2 = (pred[256]{0:T(512)(128)(4,1)S(1)}, pred[256]{0:T(512)(128)(4,1)}, u32[]{:S(2)}) copy-start(pred[256]{0:T(512)(128)(4,1)} %constant.40.clone.1) | copy-start | bytes 772
  186.9 3.7 %copy-start.1 = (bf16[4,128,128]{2,1,0:T(8,128)(2,1)S(1)}, bf16[4,128,128]{2,1,0:T(8,128)(2,1)}, u32[]{:S(2)}) copy-start(bf16[4,128,128]{2,1,0:T(8,128)(2,1)} %get-tuple-element.19) | copy-start | bytes 393220
where the time goes:
time: 194 us; the launch traced here: 191 us
  matrix products  84.3 us (43%)
  Pallas kernels  54.9 us (28%)
  other arithmetic  23.6 us (12%)
  local copies, waits for them, and re-layouts  19 us (10%)
  waiting for transfers between devices  4.88 us (3%)
  starting transfers between devices  3.63 us (2%)
    pallas_call x1, Pallas kernels, product(): pl.pallas_call(product_kernel, out_shape=(jax.ShapeDtypeStruct((NC // 4,...  54.9 us
    dot_general x1, matrix products, place_cubes(): jnp.einsum('zkby,kxb->zxy', along_z, pick_x, precision=lax.Precision.HIGH...  48 us
    dot_general x1, matrix products, place_cubes(): jnp.einsum('kza,kaby->zkby', pick_z, along_y, precision=lax.Precision.HIG...  28.5 us
    add x2, other arithmetic, fold_rims(): centre + jnp.concatenate([lower_rim, filler], axis=along_dim)  11.4 us
    dot_general x1, matrix products, place_cubes(): jnp.einsum('kabt,kyt->kaby', cube_values, pick_y, precision=lax.Precision...  7.8 us
    concatenate x1, other arithmetic, extended(): x = jnp.concatenate([before, x, after], axis=dim)  7.15 us
    concatenate x3, local copies, waits for them, and re-layouts, local(): jnp.concatenate([own, jnp.concatenate([zero, below], 1), jnp.concatenate(...  4.32 us
  transfers between devices with their start and end apart: 4, of which 3 were waited for; matrix products, arithmetic and copies ran while one was open for 2% of the time, Pallas kernels for 0%

commit v1 on v0

--- a/solution.py
+++ b/solution.py
@@ -327,49 +327,180 @@
     )(x, y, left, right, block, live, factor, anchor)
 
 
-def extended(x, sides, width):
-    for axis, dim in sides:
-        peers, length = (lax.axis_size(axis), x.shape[dim])
-        up = [(i, (i + 1) % peers) for i in range(peers)]
-        down = [(j, i) for i, j in up]
-        last = lax.slice_in_dim(x, length - width, length, axis=dim)
-        first = lax.slice_in_dim(x, 0, width, axis=dim)
-        before = lax.ppermute(last, axis, up)
-        after = lax.ppermute(first, axis, down)
-        x = jnp.concatenate([before, x, after], axis=dim)
-    return x
-
-
-def fold_rims(grown_brick, along_dim, inner_len, rim_width):
-    extent = grown_brick.shape[along_dim]
-    centre = lax.slice_in_dim(grown_brick, 2 * rim_width, 2 * rim_width + inner_len, axis=along_dim)
-    lower_rim = lax.slice_in_dim(grown_brick, 0, rim_width, axis=along_dim)
-    upper_rim = lax.slice_in_dim(grown_brick, extent - rim_width, extent, axis=along_dim)
-    pad_shape = list(lower_rim.shape)
-    pad_shape[along_dim] = inner_len - rim_width
-    filler = jnp.zeros(tuple(pad_shape), jnp.float32)
-    return (
-        centre
-        + jnp.concatenate([lower_rim, filler], axis=along_dim)
-        + jnp.concatenate([filler, upper_rim], axis=along_dim)
-    )
-
-
-def place_cubes(cube_values, corner, nz, nxy):
-    offsets = jnp.arange(CUBE, dtype=jnp.int32)
-    z_cells = jnp.arange(nz, dtype=jnp.int32)
-    xy_cells = jnp.arange(nxy, dtype=jnp.int32)
-    pick_z, pick_x, pick_y = (
-        (cells[None, :, None] == corner[:, i][:, None, None] + offsets[None, None, :]).astype(jnp.float32)
-        for i, cells in enumerate((z_cells, xy_cells, xy_cells))
-    )
-    along_y = jnp.einsum("kabt,kyt->kaby", cube_values, pick_y, precision=lax.Precision.HIGHEST)
-    along_z = jnp.einsum("kza,kaby->zkby", pick_z, along_y, precision=lax.Precision.HIGHEST)
-    return jnp.einsum("zkby,kxb->zxy", along_z, pick_x, precision=lax.Precision.HIGHEST)
+ROWS = BXY + 32
+
+
+def spread_tiles(own_ref, below_ref, above_ref, tiles):
+    lane = lax.broadcasted_iota(jnp.int32, (8, 128), 1)
+    here = lax.rem(lane // 8, 8) == lax.broadcasted_iota(jnp.int32, (8, 128), 0)
+    src = lax.broadcasted_iota(jnp.int32, (128, 256), 0)
+    dst = lax.broadcasted_iota(jnp.int32, (128, 256), 1)
+    fold = ((src // 64 == dst // 128) & (lax.rem(src, 8) == lax.rem(dst, 8))).astype(BF16)
+
+    @pl.loop(0, own_ref.shape[0])
+    def _(s):
+        for i in range(4):
+            got = (own_ref[s, i] if i < 2 else (below_ref, above_ref)[i - 2][s]).astype(F32)
+            wide = jnp.concatenate([jnp.where(here, got[j : j + 1], 0.0) for j in range(16)], axis=0)
+            out = jnp.dot(wide.astype(BF16), fold, preferred_element_type=F32)
+            for q in range(2):
+                for r in range(8):
+                    for w in range(2):
+                        tiles[i, q * 2 + w, r, s] = out[(q * 8 + r) * 8 : (q * 8 + r) * 8 + 8, w * 128 : w * 128 + 128]
+
+
+def each_cube(anchor_ref, near_ref, visit):
+    @pl.loop(0, anchor_ref.shape[2])
+    def _(k):
+        visit([(a // 4, a % 4, a - 4) for a in range(8)], k, anchor_ref[0, 0, k], anchor_ref[1, 0, k], anchor_ref[2, 0, k])
+
+        @pl.when(near_ref[0, 0, 0, k] > BZ - HALO)
+        def _():
+            visit([(2, w, w - BZ) for w in range(4)], k, near_ref[0, 0, 0, k], near_ref[0, 1, 0, k], near_ref[0, 2, 0, k])
+
+        @pl.when(near_ref[1, 0, 0, k] < HALO)
+        def _():
+            visit([(3, w, w - HALO + BZ) for w in range(4)], k, near_ref[1, 0, 0, k], near_ref[1, 1, 0, k], near_ref[1, 2, 0, k])
+
+
+def plane(z):
+    return jnp.where((z >= 0) & (z < BZ), z, BZ)
+
+
+def add_cube(out, tiles, parts, k, oz, oy, row):
+    y = oy - HALO
+    lane = lax.broadcasted_iota(jnp.int32, (8, 128), 1)
+    shift = lax.rem(y + 8, 8)
+    turned = [pltpu.roll(tiles[i, w, k // 8, lax.rem(k, 8)], shift, 1) for i, w, _ in parts]
+
+    def into(h):
+        t = lane + h * 128 - y
+        inside = (t >= 0) & (t < 8)
+        at = [(h, plane(oz + dz), pl.ds(row, 8)) for _, _, dz in parts]
+        old = [out[i] for i in at]
+        new = [o + jnp.where(inside, u, 0.0) for o, u in zip(old, turned)]
+        for i, v in zip(at, new):
+            out[i] = v
+
+    first = jnp.maximum(y, 0) // 128
+    last = jnp.minimum(y + 7, BXY - 1) // 128
+    into(first)
+
+    @pl.when(first != last)
+    def _():
+        into(last)
+
+
+def rim_kernel(anchor_ref, near_ref, own_ref, below_ref, above_ref, low_ref, high_ref, sides_ref, tiles, low, high, sides):
+    low[...] = jnp.zeros_like(low)
+    high[...] = jnp.zeros_like(high)
+    sides[...] = jnp.zeros_like(sides)
+    spread_tiles(own_ref, below_ref, above_ref, tiles)
+    lane = lax.broadcasted_iota(jnp.int32, (8, 128), 1)
+
+    def visit(parts, k, oz, ox, oy):
+        @pl.when(ox < HALO)
+        def _():
+            add_cube(low, tiles, parts, k, oz, oy, ox + 4)
+
+        @pl.when(ox > BXY - HALO)
+        def _():
+            add_cube(high, tiles, parts, k, oz, oy, ox - HALO - (BXY - 8))
+
+        @pl.when((oy < HALO) | (oy > BXY - HALO))
+        def _():
+            for i, w, dz in parts:
+                z = oz + dz
+                start = jnp.where(oy < HALO, z * 4, 64 + z * 4)
+                base = start + jnp.where(oy < HALO, oy, oy - (BXY + HALO))
+                u = pltpu.roll(tiles[i, w, k // 8, lax.rem(k, 8)], lax.rem(base + 128, 8), 1)
+                t = lane - base
+                inside = (t >= 0) & (t < 8) & (lane >= start) & (lane < start + 4) & (z >= 0) & (z < BZ)
+                rows = pl.ds(ox + 12, 8)
+                sides[rows, :] += jnp.where(inside, u, 0.0)
+
+    each_cube(anchor_ref, near_ref, visit)
+    for z in range(BZ):
+        low_ref[z] = jnp.concatenate([low[0, z, 0:8], low[1, z, 0:8]], axis=0).astype(BF16)
+        high_ref[z] = jnp.concatenate([high[0, z, 8:16], high[1, z, 8:16]], axis=0).astype(BF16)
+    sides_ref[...] = sides[...].astype(BF16)
+
+
+def exchange_kernel(low_ref, high_ref, sides_ref, low_out, high_out, sides_out, low_in, high_in, sides_in, send_sem, recv_sem):
+    nr, nc = lax.axis_size("row"), lax.axis_size("col")
+    r, c, d = lax.axis_index("row"), lax.axis_index("col"), lax.axis_index("depth")
+    barrier = pltpu.get_barrier_semaphore()
+    for i in (nr - 1, 0, 1):
+        for j in (nc - 1, 0, 1):
+            if i or j:
+                to = (lax.rem(r + i, nr), lax.rem(c + j, nc), d)
+                pl.semaphore_signal(barrier, inc=1, device_id=to, device_id_type=MESH)
+    pl.semaphore_wait(barrier, 8)
+    first, middle, last = pl.ds(0, 16), pl.ds(16, BXY), pl.ds(16 + BXY, 16)
+    plan = [
+        (0, nc - 1, sides_ref.at[middle], sides_in.at[1, middle]),
+        (0, 1, sides_ref.at[middle], sides_in.at[0, middle]),
+        (nr - 1, 0, low_ref, low_in),
+        (1, 0, high_ref, high_in),
+        (nr - 1, nc - 1, sides_ref.at[first], sides_in.at[1, last]),
+        (nr - 1, 1, sides_ref.at[first], sides_in.at[0, last]),
+        (1, nc - 1, sides_ref.at[last], sides_in.at[1, first]),
+        (1, 1, sides_ref.at[last], sides_in.at[0, first]),
+    ]
+    copies = []
+    for n, (i, j, src, dst) in enumerate(plan):
+        copy = pltpu.make_async_remote_copy(
+            src_ref=src, dst_ref=dst, send_sem=send_sem.at[n], recv_sem=recv_sem.at[n],
+            device_id=(lax.rem(r + i, nr), lax.rem(c + j, nc), d), device_id_type=MESH,
+        )
+        copy.start()
+        copies.append(copy)
+    for copy in copies:
+        copy.wait()
+    low_out[...] = low_in[...]
+    high_out[...] = high_in[...]
+    lane = lax.broadcasted_iota(jnp.int32, (BXY, 128), 1)
+    sides = jnp.where(lane < 64, sides_in[1, middle, :].astype(F32), sides_in[0, middle, :].astype(F32))
+    sides_out[...] = sides
+    for at, rows in ((first, pl.ds(0, 8)), (last, pl.ds(BXY - 8, 8))):
+        got = jnp.where(
+            lax.broadcasted_iota(jnp.int32, (16, 128), 1) < 64, sides_in[1, at, :].astype(F32), sides_in[0, at, :].astype(F32)
+        )
+        sides_out[rows, :] += got[0:8] if at is first else got[8:16]
+
+
+def brick_kernel(anchor_ref, near_ref, own_ref, below_ref, above_ref, low_ref, high_ref, sides_ref, density_ref, density_out, charge_ref, tiles, brick, sems):
+    copy = pltpu.make_async_copy(density_ref, density_out, sems.at[2])
+    copy.start()
+    src = lax.broadcasted_iota(jnp.int32, (128, 256), 0)
+    dst = lax.broadcasted_iota(jnp.int32, (128, 256), 1)
+    sides = sides_ref[...].astype(BF16)
+
+    @pl.loop(0, BZ)
+    def _(z):
+        unfold = (((dst < 4) & (src == 64 + z * 4 + dst)) | ((dst >= BXY - 4) & (src == z * 4 + dst - (BXY - 4)))).astype(BF16)
+        out = jnp.dot(sides, unfold, preferred_element_type=F32)
+        for h in range(2):
+            brick[h, z, 16 : 16 + BXY, :] = out[:, h * 128 : h * 128 + 128]
+            brick[h, z, 16:24, :] += high_ref[z].astype(F32)[8 * h : 8 * h + 8]
+            brick[h, z, 8 + BXY : 16 + BXY, :] += low_ref[z].astype(F32)[8 * h : 8 * h + 8]
+
+    spread_tiles(own_ref, below_ref, above_ref, tiles)
+    each_cube(anchor_ref, near_ref, lambda parts, k, oz, ox, oy: add_cube(brick, tiles, parts, k, oz, oy, ox + 12))
+    copies = [
+        pltpu.make_async_copy(brick.at[h, pl.ds(0, BZ), pl.ds(16, BXY)], charge_ref.at[:, :, pl.ds(h * 128, 128)], sems.at[h])
+        for h in range(2)
+    ]
+    for x in copies:
+        x.start()
+    for x in copies:
+        x.wait()
+    copy.wait()
 
 
 def local(x_blocks, y_blocks, task_left, task_right, colloc_block, live, factors, cube_anchor):
     nr, nc = lax.axis_size("row"), lax.axis_size("col")
+    anchor = cube_anchor[0, 0, 0, :, 0, :].T.reshape(3, 1, -1)
     density, own, below, above, near = product(
         x_blocks.reshape(NA * BLK, BLK),
         y_blocks.reshape(NB * BLK, BLK),
@@ -378,21 +509,57 @@
         colloc_block.reshape(-1),
         live.reshape(-1),
         factors.reshape(-1, BLK),
-        cube_anchor[0, 0, 0],
+        anchor,
         nr, nc,
     )
-    zero = jnp.zeros((64, 256), F32)
-    own = own.astype(F32).reshape(nc, 2, 2, 8, 128).transpose(3, 0, 1, 2, 4).reshape(64, 512)
-    below = below.astype(F32).reshape(nc, 2, 8, 128).transpose(2, 0, 1, 3).reshape(64, 256)
-    above = above.astype(F32).reshape(nc, 2, 8, 128).transpose(2, 0, 1, 3).reshape(64, 256)
-    values = jnp.concatenate([own, jnp.concatenate([zero, below], 1), jnp.concatenate([above, zero], 1)], 0)
-    corner = jnp.concatenate([cube_anchor.reshape(-1, 3), near[0].reshape(-1, 3), near[1].reshape(-1, 3)], 0)
-    shift = jnp.concatenate([jnp.full((64,), -4), jnp.full((64,), -20), jnp.full((64,), 12)]).astype(jnp.int32)
-    corner = corner.at[:, 0].add(shift)
-    brick = place_cubes(values.reshape(-1, CUBE, CUBE, CUBE), corner, BZ, BXY + 2 * HALO)
-    grown_brick = extended(brick, (("row", 1), ("col", 2)), HALO)
-    charge = fold_rims(grown_brick, 1, BXY, HALO)
-    charge = fold_rims(charge, 2, BXY, HALO)
+    vmem = pl.BlockSpec(memory_space=pltpu.VMEM)
+    smem = pl.BlockSpec(memory_space=pltpu.SMEM)
+    hbm = pl.BlockSpec(memory_space=pl.ANY)
+    dma = pltpu.SemaphoreType.DMA
+    tiles = pltpu.VMEM((4, 4, 8, nc, 8, 128), F32)
+    params = functools.partial(pltpu.CompilerParams, vmem_limit_bytes=48 * 1024 * 1024)
+    faces = (jax.ShapeDtypeStruct((BZ, 16, 128), BF16),) * 2
+    low, high, sides = pl.pallas_call(
+        rim_kernel,
+        out_shape=(*faces, jax.ShapeDtypeStruct((ROWS, 128), BF16)),
+        in_specs=[smem, smem, vmem, vmem, vmem],
+        out_specs=(vmem, vmem, vmem),
+        scratch_shapes=[
+            tiles,
+            pltpu.VMEM((2, BZ + 1, 16, 128), F32),
+            pltpu.VMEM((2, BZ + 1, 16, 128), F32),
+            pltpu.VMEM((ROWS, 128), F32),
+        ],
+        compiler_params=params(),
+        name="rims",
+    )(anchor, near, own, below, above)
+    low, high, sides = pl.pallas_call(
+        exchange_kernel,
+        out_shape=(*faces, jax.ShapeDtypeStruct((BXY, 128), F32)),
+        in_specs=[vmem, vmem, vmem],
+        out_specs=(vmem, vmem, vmem),
+        scratch_shapes=[
+            pltpu.VMEM((BZ, 16, 128), BF16),
+            pltpu.VMEM((BZ, 16, 128), BF16),
+            pltpu.VMEM((2, ROWS, 128), BF16),
+            dma((8,)),
+            dma((8,)),
+        ],
+        compiler_params=params(collective_id=1, has_side_effects=True),
+        name="rim_exchange",
+    )(low, high, sides)
+    density, charge = pl.pallas_call(
+        brick_kernel,
+        out_shape=(
+            jax.ShapeDtypeStruct(density.shape, BF16),
+            jax.ShapeDtypeStruct((BZ, BXY, BXY), F32),
+        ),
+        in_specs=[smem, smem, vmem, vmem, vmem, vmem, vmem, vmem, hbm],
+        out_specs=(hbm, hbm),
+        scratch_shapes=[tiles, pltpu.VMEM((2, BZ + 1, ROWS, 128), F32), dma((3,))],
+        compiler_params=params(),
+        name="brick",
+    )(anchor, near, own, below, above, low, high, sides, density)
     return (density[None, None], charge)
 
 

time: 194 us -> 96.1 us (0.50); the launches traced: 191 us -> 95.5 us
  matrix products: 84.3 us -> 0 us
  Pallas kernels: 54.9 us -> 85.9 us
  other arithmetic: 23.6 us -> 0 us
  local copies, waits for them, and re-layouts: 19 us -> 8.89 us
  waiting for transfers between devices: 4.88 us -> 0 us
  starting transfers between devices: 3.63 us -> 0 us
    dot_general x3 -> x0, matrix products: 84.3 us -> none  [the longest x1 48 us: place_cubes(): jnp.einsum('zkby,kxb->zxy', along_z, pick_x, precision=lax.Precision.HIGH...]
    pallas_call x0 -> x3, Pallas kernels: none -> 31 us  [the longest x1 15.4 us: local(): pl.pallas_call(brick_kernel, out_shape=(jax.ShapeDtypeStruct(density.shap...]
    add x5 -> x0, other arithmetic: 11.6 us -> none  [the longest x2 11.4 us: fold_rims(): centre + jnp.concatenate([lower_rim, filler], axis=along_dim)]
    concatenate x2 -> x0, other arithmetic: 7.88 us -> none  [the longest x1 7.15 us: extended(): x = jnp.concatenate([before, x, after], axis=dim)]
    unnamed x15 -> x21, local copies, waits for them, and re-layouts: 2.97 us -> 8.32 us
    slice x5 -> x0, local copies, waits for them, and re-layouts: 4.88 us -> none  [the longest x1 2.54 us: extended(): first = lax.slice_in_dim(x, 0, width, axis=dim)]
    ppermute x4 -> x0, waiting for transfers between devices: 4.88 us -> none  [the longest x2 3.02 us: extended(): after = lax.ppermute(first, axis, down)]
    concatenate x5 -> x0, local copies, waits for them, and re-layouts: 4.37 us -> none  [the longest x3 4.32 us: local(): jnp.concatenate([own, jnp.concatenate([zero, below], 1), jnp.concatenate(...]
  transfers between devices with their start and end apart: 4 -> 0, of which waited for: 3 -> 0; matrix products, arithmetic and copies ran while one was open for 2% -> 0% of each run, Pallas kernels for 0% -> 0%
where the time goes in v1:
time: 96.1 us; the launch traced here: 95.5 us
  Pallas kernels  85.9 us (89%)
  local copies, waits for them, and re-layouts  8.89 us (9%)
    pallas_call x1, Pallas kernels, product(): pl.pallas_call(product_kernel, out_shape=(jax.ShapeDtypeStruct((NC // 4,...  54.9 us
    pallas_call x1, Pallas kernels, local(): pl.pallas_call(brick_kernel, out_shape=(jax.ShapeDtypeStruct(density.shap...  15.4 us
    pallas_call x1, Pallas kernels, local(): pl.pallas_call(exchange_kernel, out_shape=(*faces, jax.ShapeDtypeStruct((...  8.58 us
    unnamed x21, local copies, waits for them, and re-layouts  8.32 us
    pallas_call x1, Pallas kernels, local(): pl.pallas_call(rim_kernel, out_shape=(*faces, jax.ShapeDtypeStruct((ROWS,...  6.99 us

profile of v1, /device:TPU:1, one launch (start us, length us, event | category | flops | bytes accessed | tf_op | source)
XLA Modules:
  0.0 95.5 jit_solution(14518452794286887532)
XLA Ops:
  0.6 0.7 copy.12
  1.3 0.6 reshape.22.anchor_ref
  1.9 54.9 %product_and_cubes.1 = (bf16[4,128,128]{2,1,0:T(8,128)(2,1)}, bf16[8,2,16,128]{3,2,1,0:T(8,128)(2,1)}, bf16[8,16,128]{2,1,0:T(8,128)(2,1)}, bf16[8,16,128]{2,1,0:T(8,128)(2,1)}, s32[2,3,1,64]{3,2,1,0:T(1,128)}) custom-call(bf16[256,128]{1,0:T(8,128)(2,1)} %bitcast.15, bf16[512,128]{1,0:T(8,128)(2,1)} %bitcast.14, s32[8,8,16]{2,1,0:T(8,128)} %bitcast.16, ...), custom_call_target="tpu_custom_call" | custom-call | tf_op jit(solution)/shard_map/product_and_cubes/pallas_call | solution.py:293
  56.8 0.0 copy-start
  56.8 0.8 copy-done
  57.7 0.0 copy-start.3
  57.7 0.8 copy-done.3
  58.4 0.0 copy-start.5
  58.4 0.8 copy-done.5
  59.2 0.0 copy-start.7
  59.2 0.7 copy-done.7
  59.9 0.0 copy-start.8
  59.9 0.7 copy-done.8
  60.6 7.0 %rims.1 = (bf16[16,16,128]{2,1,0:T(8,128)(2,1)S(1)}, bf16[16,16,128]{2,1,0:T(8,128)(2,1)S(1)}, bf16[288,128]{1,0:T(8,128)(2,1)S(1)}) custom-call(s32[3,1,64]{2,1,0:T(1,128)S(1)} %copy-done.7, s32[2,3,1,64]{3,2,1,0:T(1,128)S(1)} %copy-done.8, bf16[8,2,16,128]{3,2,1,0:T(8,128)(2,1)S(1)} %copy-done, bf16[8,16,128]{2,1,0:T(8,128)(2,1)S(1)} %copy-done.3, ...), custom_call_target="tpu_custom_call" | custom-call | tf_op jit(solution)/shard_map/rims/pallas_call | solution.py:522
  67.5 8.6 %rim_exchange.1 = (bf16[16,16,128]{2,1,0:T(8,128)(2,1)S(1)}, bf16[16,16,128]{2,1,0:T(8,128)(2,1)S(1)}, f32[256,128]{1,0:T(8,128)S(1)}) custom-call(bf16[16,16,128]{2,1,0:T(8,128)(2,1)S(1)} %get-tuple-element.19.low_ref, bf16[16,16,128]{2,1,0:T(8,128)(2,1)S(1)} %get-tuple-element.20.high_ref, bf16[288,128]{1,0:T(8,128)(2,1)S(1)} %get-tuple-element.21.sides_ref), custom_call_target="tpu_custom_call" | custom-call | tf_op jit(solution)/shard_map/rim_exchange/pallas_call | solution.py:536
  76.1 0.0 copy-start.1
  76.1 0.8 copy-done.1
  77.0 0.0 copy-start.2
  77.0 0.9 copy-done.2
  77.9 0.0 copy-start.4
  77.9 0.8 copy-done.4
  78.6 0.0 copy-start.6
  78.6 0.8 copy-done.6
  79.4 0.0 copy-start.9
  79.4 0.7 copy-done.9
  80.1 15.4 %brick.1 = (bf16[4,128,128]{2,1,0:T(8,128)(2,1)}, f32[16,256,256]{2,1,0:T(8,128)}) custom-call(s32[3,1,64]{2,1,0:T(1,128)S(1)} %copy-done.7, s32[2,3,1,64]{3,2,1,0:T(1,128)S(1)} %copy-done.9, bf16[8,2,16,128]{3,2,1,0:T(8,128)(2,1)S(1)} %copy-done.1, bf16[8,16,128]{2,1,0:T(8,128)(2,1)S(1)} %copy-done.4, bf16[8,16,128]{2,1,0:T(8,128)(2,1)S(1)} %copy-done.6, ...), custom_call_target="tpu_custom_call" | custom-call | tf_op jit(solution)/shard_map/brick/pallas_call | solution.py:551
Async XLA Ops:
  56.8 0.8 copy-start
  57.7 0.8 copy-start.3
  58.4 0.8 copy-start.5
  59.2 0.7 copy-start.7
  59.9 0.7 copy-start.8
  76.1 0.8 copy-start.1
  77.0 0.9 copy-start.2
  77.9 0.8 copy-start.4
  78.6 0.8 copy-start.6
  79.4 0.7 copy-start.9

commit v2 on v1

--- a/solution.py
+++ b/solution.py
@@ -24,12 +24,13 @@
 
 
 def product_kernel(
-    x_ref, y_ref, left_ref, right_ref, block_ref, live_ref, factor_ref, anchor_ref,
-    density_ref, own_ref, below_ref, above_ref, near_anchor_ref,
+    x_hbm, y_hbm, left_hbm, right_hbm, block_ref, live_ref, factor_hbm, anchor_ref,
+    density_ref, own_ref, below_ref, above_ref, near_ref,
+    x_ref, y_ref, left_ref, right_ref, factor_ref, near_anchor_ref,
     xg, yg, kmat, rhs, total, part_out, part_in, b0, b1, pairs, cubes, first_in, second_out,
     own_in, below_in, above_in,
     xr_send, xr_recv, xl_send, xl_recv, yr_send, yr_recv, yl_send, yl_recv, ys_send, ys_recv,
-    part_send, part_recv, first_send, first_recv, second_send, second_recv, anchor_send, anchor_recv,
+    part_send, part_recv, first_send, first_recv, second_send, second_recv, anchor_send, anchor_recv, load_sem,
 ):
     nr, nc, nd = lax.axis_size("row"), lax.axis_size("col"), lax.axis_size("depth")
     chips = nr // 2
@@ -61,6 +62,11 @@
     for k in range(2, nd - 1):
         pl.semaphore_signal(barrier, inc=1, device_id=(r, c, up(d, k, nd)), device_id_type=MESH)
         greeted += 1
+    loads = [pltpu.make_async_copy(a, b, load_sem.at[i]) for i, (a, b) in enumerate(((x_hbm, x_ref), (y_hbm, y_ref), (left_hbm, left_ref), (right_hbm, right_ref), (factor_hbm, factor_ref)))]
+    for load in loads:
+        load.start()
+    loads[0].wait()
+    loads[1].wait()
     pl.semaphore_wait(barrier, greeted)
 
     copies = []
@@ -101,6 +107,8 @@
     for i, k in enumerate((1, nd - 1)):
         copies.append(send(anchor_ref, near_anchor_ref.at[i], anchor_send.at[i], anchor_recv.at[i], r, c, up(d, k, nd)))
 
+    loads[2].wait()
+    loads[3].wait()
     npair = NA * NB
     task = left_ref[...] * NB + right_ref[...]
     counts = jnp.concatenate(
@@ -164,6 +172,7 @@
     quarter = nslot // 8
 
     panel(0)
+    loads[4].wait()
     x_wait(1)
     x_step(2)
     y_wait(up(r, nr - 2, nr), whole, yr_recv.at[0])
@@ -182,14 +191,12 @@
     y_share(2)
     panel(2)
     panel(nr - 2)
-    basis(quarter, 2 * quarter)
     x_wait(3)
     x_step(4)
     for q in range(chips):
         y_wait(lax.rem(sibling + 2 * q, nr), whole, ys_recv.at[q])
     for delta in (1, nr - 1, 3, nr - 3):
         panel(delta)
-    basis(2 * quarter, 3 * quarter)
     x_wait(4)
     stage_panel(half)
     k = lax.rem(r + c + half, npanel)
@@ -203,7 +210,7 @@
         part_out[j - 1] = last(dest).astype(BF16)
         copies.append(send(part_out.at[j - 1], part_in.at[j - 1], part_send.at[j - 1], part_recv.at[j - 1], r, c, dest))
     summed = last(d)
-    basis(3 * quarter, 4 * quarter)
+    basis(quarter, 4 * quarter)
     for j in (1, 3, 2):
         pltpu.make_async_copy(part_in.at[j - 1], part_in.at[j - 1], part_recv.at[j - 1]).wait()
         summed = summed + part_in[j - 1].astype(F32)
@@ -239,7 +246,7 @@
                 new.append(acc[q] + lax.dot_general(ones, v, NT, preferred_element_type=F32))
             return tuple(new)
 
-        acc = lax.fori_loop(0, 8, two, tuple(jnp.zeros((16, 128), F32) for _ in range(4)))
+        acc = lax.fori_loop(0, 8, two, tuple(jnp.zeros((16, 128), F32) for _ in range(4)), unroll=4)
         for q in range(4):
             cubes[j, q] = acc[q]
         for w in range(2):
@@ -280,6 +287,8 @@
         above_ref[s] = above_in[s]
     for i in range(2):
         pltpu.make_async_copy(near_anchor_ref.at[i], near_anchor_ref.at[i], anchor_recv.at[i]).wait()
+        near_ref[i + 1] = near_anchor_ref[i]
+    near_ref[0] = anchor_ref[...]
     for copy in copies:
         copy.wait_send()
 
@@ -293,15 +302,21 @@
     return pl.pallas_call(
         product_kernel,
         out_shape=(
-            jax.ShapeDtypeStruct((NC // 4, BLK, BLK), BF16),
-            jax.ShapeDtypeStruct((nc, 2, 16, 128), BF16),
-            jax.ShapeDtypeStruct((nc, 16, 128), BF16),
-            jax.ShapeDtypeStruct((nc, 16, 128), BF16),
-            jax.ShapeDtypeStruct((2, *anchor.shape), jnp.int32),
+            pltpu.VMEM((NC // 4, BLK, BLK), BF16),
+            pltpu.VMEM((nc, 2, 16, 128), BF16),
+            pltpu.VMEM((nc, 16, 128), BF16),
+            pltpu.VMEM((nc, 16, 128), BF16),
+            pltpu.VMEM((3, *anchor.shape), jnp.int32),
         ),
-        in_specs=[vmem, vmem, vmem, vmem, smem, smem, vmem, hbm],
-        out_specs=(vmem, vmem, vmem, vmem, hbm),
+        in_specs=[hbm, hbm, hbm, hbm, smem, smem, hbm, vmem],
+        out_specs=(vmem,) * 5,
         scratch_shapes=[
+            pltpu.VMEM(x.shape, BF16),
+            pltpu.VMEM(y.shape, BF16),
+            pltpu.VMEM(left.shape, jnp.int32),
+            pltpu.VMEM(right.shape, jnp.int32),
+            pltpu.VMEM(factor.shape, BF16),
+            pltpu.VMEM((2, *anchor.shape), jnp.int32),
             pltpu.VMEM((nc, 256, 128), BF16),
             pltpu.VMEM((nr, 512, 128), BF16),
             pltpu.VMEM((8, 256, 256), BF16),
@@ -320,7 +335,7 @@
             pltpu.VMEM((nc, 16, 128), BF16),
             dma((4,)), dma((4,)), dma((4,)), dma((4,)),
             dma((2,)), dma((2,)), dma((2,)), dma((2,)), dma((4,)), dma((4,)),
-            dma((3,)), dma((3,)), dma((8,)), dma((8,)), dma((3, 8)), dma((3, 8)), dma((2,)), dma((2,)),
+            dma((3,)), dma((3,)), dma((8,)), dma((8,)), dma((3, 8)), dma((3, 8)), dma((2,)), dma((2,)), dma((5,)),
         ],
         compiler_params=pltpu.CompilerParams(collective_id=0, has_side_effects=True, vmem_limit_bytes=56 * 1024 * 1024),
         name="product_and_cubes",
@@ -330,82 +345,65 @@
 ROWS = BXY + 32
 
 
-def spread_tiles(own_ref, below_ref, above_ref, tiles):
+def spread_tiles(anchor_ref, near_ref, own_ref, below_ref, above_ref, tiles):
+    row16 = lax.broadcasted_iota(jnp.int32, (16, 128), 0)
+    lane16 = lax.broadcasted_iota(jnp.int32, (16, 128), 1)
     lane = lax.broadcasted_iota(jnp.int32, (8, 128), 1)
     here = lax.rem(lane // 8, 8) == lax.broadcasted_iota(jnp.int32, (8, 128), 0)
     src = lax.broadcasted_iota(jnp.int32, (128, 256), 0)
     dst = lax.broadcasted_iota(jnp.int32, (128, 256), 1)
     fold = ((src // 64 == dst // 128) & (lax.rem(src, 8) == lax.rem(dst, 8))).astype(BF16)
 
+    def turn(corner, s):
+        y = jnp.zeros((16, 128), jnp.int32)
+        for r in range(8):
+            y = jnp.where(lax.rem(row16, 8) == r, corner(r * 8 + s) - HALO, y)
+        return lane16 - lax.rem(lane16, 8) + lax.rem(lane16 - y + BXY * 2, 8)
+
     @pl.loop(0, own_ref.shape[0])
     def _(s):
-        for i in range(4):
-            got = (own_ref[s, i] if i < 2 else (below_ref, above_ref)[i - 2][s]).astype(F32)
+        index = turn(lambda k: anchor_ref[2, 0, k], s)
+        parts = [(own_ref[s, 0], index), (own_ref[s, 1], index)]
+        parts.append((below_ref[s], turn(lambda k: near_ref[0, 2, 0, k], s)))
+        parts.append((above_ref[s], turn(lambda k: near_ref[1, 2, 0, k], s)))
+        for i, (got, index) in enumerate(parts):
+            got = got.astype(F32)
+            got = jnp.concatenate(
+                [jnp.take_along_axis(got[j : j + 8], index[j : j + 8], axis=1) for j in (0, 8)], axis=0
+            )
             wide = jnp.concatenate([jnp.where(here, got[j : j + 1], 0.0) for j in range(16)], axis=0)
             out = jnp.dot(wide.astype(BF16), fold, preferred_element_type=F32)
             for q in range(2):
                 for r in range(8):
                     for w in range(2):
-                        tiles[i, q * 2 + w, r, s] = out[(q * 8 + r) * 8 : (q * 8 + r) * 8 + 8, w * 128 : w * 128 + 128]
-
-
-def each_cube(anchor_ref, near_ref, visit):
-    @pl.loop(0, anchor_ref.shape[2])
-    def _(k):
-        visit([(a // 4, a % 4, a - 4) for a in range(8)], k, anchor_ref[0, 0, k], anchor_ref[1, 0, k], anchor_ref[2, 0, k])
-
-        @pl.when(near_ref[0, 0, 0, k] > BZ - HALO)
-        def _():
-            visit([(2, w, w - BZ) for w in range(4)], k, near_ref[0, 0, 0, k], near_ref[0, 1, 0, k], near_ref[0, 2, 0, k])
-
-        @pl.when(near_ref[1, 0, 0, k] < HALO)
-        def _():
-            visit([(3, w, w - HALO + BZ) for w in range(4)], k, near_ref[1, 0, 0, k], near_ref[1, 1, 0, k], near_ref[1, 2, 0, k])
-
-
-def plane(z):
-    return jnp.where((z >= 0) & (z < BZ), z, BZ)
-
-
-def add_cube(out, tiles, parts, k, oz, oy, row):
-    y = oy - HALO
+                        tiles[i, q * 2 + w, r * 8 + s] = out[(q * 8 + r) * 8 : (q * 8 + r) * 8 + 8, w * 128 : w * 128 + 128]
+
+
+def place_kernel(corner_ref, own_ref, below_ref, above_ref, brick, low_ref, high_ref, sides_ref, tiles, sides):
+    anchor_ref, near_ref = corner_ref.at[0], corner_ref.at[pl.ds(1, 2)]
+    for h in range(2):
+
+        @pl.loop(0, BZ)
+        def _(z):
+            brick[h, z, 8 : 24 + BXY, :] = jnp.zeros((16 + BXY, 128), F32)
+
+    sides[...] = jnp.zeros_like(sides)
+    spread_tiles(anchor_ref, near_ref, own_ref, below_ref, above_ref, tiles)
     lane = lax.broadcasted_iota(jnp.int32, (8, 128), 1)
-    shift = lax.rem(y + 8, 8)
-    turned = [pltpu.roll(tiles[i, w, k // 8, lax.rem(k, 8)], shift, 1) for i, w, _ in parts]
-
-    def into(h):
-        t = lane + h * 128 - y
-        inside = (t >= 0) & (t < 8)
-        at = [(h, plane(oz + dz), pl.ds(row, 8)) for _, _, dz in parts]
-        old = [out[i] for i in at]
-        new = [o + jnp.where(inside, u, 0.0) for o, u in zip(old, turned)]
-        for i, v in zip(at, new):
-            out[i] = v
-
-    first = jnp.maximum(y, 0) // 128
-    last = jnp.minimum(y + 7, BXY - 1) // 128
-    into(first)
-
-    @pl.when(first != last)
-    def _():
-        into(last)
-
-
-def rim_kernel(anchor_ref, near_ref, own_ref, below_ref, above_ref, low_ref, high_ref, sides_ref, tiles, low, high, sides):
-    low[...] = jnp.zeros_like(low)
-    high[...] = jnp.zeros_like(high)
-    sides[...] = jnp.zeros_like(sides)
-    spread_tiles(own_ref, below_ref, above_ref, tiles)
-    lane = lax.broadcasted_iota(jnp.int32, (8, 128), 1)
-
-    def visit(parts, k, oz, ox, oy):
-        @pl.when(ox < HALO)
-        def _():
-            add_cube(low, tiles, parts, k, oz, oy, ox + 4)
-
-        @pl.when(ox > BXY - HALO)
-        def _():
-            add_cube(high, tiles, parts, k, oz, oy, ox - HALO - (BXY - 8))
+
+    def add(parts, k, oz, ox, oy):
+        first = jnp.maximum(oy - HALO, 0) // 128
+        rows = pl.ds(ox + 16 - HALO, 8)
+        for h in (first, first + 1):
+            t = lane + (h * 128 - oy + HALO)
+            inside = (t >= 0) & (t < 8)
+            at = []
+            for _, _, dz in parts:
+                z = oz + dz
+                at.append((h, jnp.where((z >= 0) & (z < BZ), z, BZ), rows))
+            new = [brick[x] + jnp.where(inside, tiles[i, w, k], 0.0) for x, (i, w, _) in zip(at, parts)]
+            for x, v in zip(at, new):
+                brick[x] = v
 
         @pl.when((oy < HALO) | (oy > BXY - HALO))
         def _():
@@ -413,16 +411,28 @@
                 z = oz + dz
                 start = jnp.where(oy < HALO, z * 4, 64 + z * 4)
                 base = start + jnp.where(oy < HALO, oy, oy - (BXY + HALO))
-                u = pltpu.roll(tiles[i, w, k // 8, lax.rem(k, 8)], lax.rem(base + 128, 8), 1)
+                u = pltpu.roll(tiles[i, w, k], lax.rem(base - oy + HALO + 512, 8), 1)
                 t = lane - base
                 inside = (t >= 0) & (t < 8) & (lane >= start) & (lane < start + 4) & (z >= 0) & (z < BZ)
-                rows = pl.ds(ox + 12, 8)
                 sides[rows, :] += jnp.where(inside, u, 0.0)
 
-    each_cube(anchor_ref, near_ref, visit)
+    @pl.loop(0, anchor_ref.shape[2])
+    def _(k):
+        add([(a // 4, a % 4, a - 4) for a in range(8)], k, anchor_ref[0, 0, k], anchor_ref[1, 0, k], anchor_ref[2, 0, k])
+
+    @pl.loop(0, anchor_ref.shape[2])
+    def _(k):
+        @pl.when(near_ref[0, 0, 0, k] > BZ - HALO)
+        def _():
+            add([(2, w, w - BZ) for w in range(4)], k, near_ref[0, 0, 0, k], near_ref[0, 1, 0, k], near_ref[0, 2, 0, k])
+
+        @pl.when(near_ref[1, 0, 0, k] < HALO)
+        def _():
+            add([(3, w, w - HALO + BZ) for w in range(4)], k, near_ref[1, 0, 0, k], near_ref[1, 1, 0, k], near_ref[1, 2, 0, k])
+
     for z in range(BZ):
-        low_ref[z] = jnp.concatenate([low[0, z, 0:8], low[1, z, 0:8]], axis=0).astype(BF16)
-        high_ref[z] = jnp.concatenate([high[0, z, 8:16], high[1, z, 8:16]], axis=0).astype(BF16)
+        low_ref[z] = jnp.concatenate([brick[h, z, 8:16] for h in range(2)], axis=0).astype(BF16)
+        high_ref[z] = jnp.concatenate([brick[h, z, 16 + BXY : 24 + BXY] for h in range(2)], axis=0).astype(BF16)
     sides_ref[...] = sides[...].astype(BF16)
 
 
@@ -469,39 +479,64 @@
         sides_out[rows, :] += got[0:8] if at is first else got[8:16]
 
 
-def brick_kernel(anchor_ref, near_ref, own_ref, below_ref, above_ref, low_ref, high_ref, sides_ref, density_ref, density_out, charge_ref, tiles, brick, sems):
-    copy = pltpu.make_async_copy(density_ref, density_out, sems.at[2])
-    copy.start()
+def charge_kernel(brick, low_ref, high_ref, sides_ref, density_ref, density_out, charge_ref, full, sems):
+    copies = [pltpu.make_async_copy(density_ref, density_out, sems.at[BZ])]
+    copies[0].start()
     src = lax.broadcasted_iota(jnp.int32, (128, 256), 0)
     dst = lax.broadcasted_iota(jnp.int32, (128, 256), 1)
     sides = sides_ref[...].astype(BF16)
-
-    @pl.loop(0, BZ)
-    def _(z):
-        unfold = (((dst < 4) & (src == 64 + z * 4 + dst)) | ((dst >= BXY - 4) & (src == z * 4 + dst - (BXY - 4)))).astype(BF16)
+    at = jnp.where(dst < 4, 64 + dst, jnp.where(dst >= BXY - 4, dst - (BXY - 4), -BXY))
+    for z in range(BZ):
+        unfold = (src == at + z * 4).astype(BF16)
         out = jnp.dot(sides, unfold, preferred_element_type=F32)
         for h in range(2):
-            brick[h, z, 16 : 16 + BXY, :] = out[:, h * 128 : h * 128 + 128]
-            brick[h, z, 16:24, :] += high_ref[z].astype(F32)[8 * h : 8 * h + 8]
-            brick[h, z, 8 + BXY : 16 + BXY, :] += low_ref[z].astype(F32)[8 * h : 8 * h + 8]
-
-    spread_tiles(own_ref, below_ref, above_ref, tiles)
-    each_cube(anchor_ref, near_ref, lambda parts, k, oz, ox, oy: add_cube(brick, tiles, parts, k, oz, oy, ox + 12))
-    copies = [
-        pltpu.make_async_copy(brick.at[h, pl.ds(0, BZ), pl.ds(16, BXY)], charge_ref.at[:, :, pl.ds(h * 128, 128)], sems.at[h])
-        for h in range(2)
-    ]
-    for x in copies:
-        x.start()
-    for x in copies:
-        x.wait()
-    copy.wait()
+            lanes = slice(h * 128, h * 128 + 128)
+            full[z, :, lanes] = out[:, lanes] + brick[h, z, 16 : 16 + BXY, :]
+            full[z, 0:8, lanes] += high_ref[z].astype(F32)[8 * h : 8 * h + 8]
+            full[z, BXY - 8 : BXY, lanes] += low_ref[z].astype(F32)[8 * h : 8 * h + 8]
+        copies.append(pltpu.make_async_copy(full.at[z], charge_ref.at[z], sems.at[z]))
+        copies[-1].start()
+    for copy in copies:
+        copy.wait()
+
+
+def place(corner, own, below, above):
+    vmem = pl.BlockSpec(memory_space=pltpu.VMEM)
+    smem = pl.BlockSpec(memory_space=pltpu.SMEM)
+    nk = corner.shape[3]
+    faces = (jax.ShapeDtypeStruct((BZ, 16, 128), BF16),) * 2
+    return pl.pallas_call(
+        place_kernel,
+        out_shape=(pltpu.VMEM((3, BZ + 1, ROWS, 128), F32), *faces, jax.ShapeDtypeStruct((ROWS, 128), BF16)),
+        in_specs=[smem, vmem, vmem, vmem],
+        out_specs=(vmem, vmem, vmem, vmem),
+        scratch_shapes=[pltpu.VMEM((4, 4, nk, 8, 128), F32), pltpu.VMEM((ROWS, 128), F32)],
+        compiler_params=pltpu.CompilerParams(vmem_limit_bytes=24 * 1024 * 1024),
+        name="place",
+    )(corner, own, below, above)
+
+
+def finish(brick, low, high, sides, density):
+    vmem = pl.BlockSpec(memory_space=pltpu.VMEM)
+    hbm = pl.BlockSpec(memory_space=pl.ANY)
+    return pl.pallas_call(
+        charge_kernel,
+        out_shape=(
+            jax.ShapeDtypeStruct(density.shape, BF16),
+            jax.ShapeDtypeStruct((BZ, BXY, BXY), F32),
+        ),
+        in_specs=[vmem, vmem, vmem, vmem, vmem],
+        out_specs=(hbm, hbm),
+        scratch_shapes=[pltpu.VMEM((BZ, BXY, BXY), F32), pltpu.SemaphoreType.DMA((BZ + 1,))],
+        compiler_params=pltpu.CompilerParams(vmem_limit_bytes=24 * 1024 * 1024),
+        name="charge",
+    )(brick, low, high, sides, density)
 
 
 def local(x_blocks, y_blocks, task_left, task_right, colloc_block, live, factors, cube_anchor):
     nr, nc = lax.axis_size("row"), lax.axis_size("col")
-    anchor = cube_anchor[0, 0, 0, :, 0, :].T.reshape(3, 1, -1)
-    density, own, below, above, near = product(
+    anchor = cube_anchor[0, 0, 0].transpose(2, 1, 0)
+    density, own, below, above, corner = product(
         x_blocks.reshape(NA * BLK, BLK),
         y_blocks.reshape(NB * BLK, BLK),
         task_left[0, 0, 0],
@@ -513,29 +548,11 @@
         nr, nc,
     )
     vmem = pl.BlockSpec(memory_space=pltpu.VMEM)
-    smem = pl.BlockSpec(memory_space=pltpu.SMEM)
-    hbm = pl.BlockSpec(memory_space=pl.ANY)
     dma = pltpu.SemaphoreType.DMA
-    tiles = pltpu.VMEM((4, 4, 8, nc, 8, 128), F32)
-    params = functools.partial(pltpu.CompilerParams, vmem_limit_bytes=48 * 1024 * 1024)
-    faces = (jax.ShapeDtypeStruct((BZ, 16, 128), BF16),) * 2
-    low, high, sides = pl.pallas_call(
-        rim_kernel,
-        out_shape=(*faces, jax.ShapeDtypeStruct((ROWS, 128), BF16)),
-        in_specs=[smem, smem, vmem, vmem, vmem],
-        out_specs=(vmem, vmem, vmem),
-        scratch_shapes=[
-            tiles,
-            pltpu.VMEM((2, BZ + 1, 16, 128), F32),
-            pltpu.VMEM((2, BZ + 1, 16, 128), F32),
-            pltpu.VMEM((ROWS, 128), F32),
-        ],
-        compiler_params=params(),
-        name="rims",
-    )(anchor, near, own, below, above)
+    brick, low, high, sides = place(corner, own, below, above)
     low, high, sides = pl.pallas_call(
         exchange_kernel,
-        out_shape=(*faces, jax.ShapeDtypeStruct((BXY, 128), F32)),
+        out_shape=(*(jax.ShapeDtypeStruct((BZ, 16, 128), BF16),) * 2, jax.ShapeDtypeStruct((BXY, 128), F32)),
         in_specs=[vmem, vmem, vmem],
         out_specs=(vmem, vmem, vmem),
         scratch_shapes=[
@@ -545,21 +562,10 @@
             dma((8,)),
             dma((8,)),
         ],
-        compiler_params=params(collective_id=1, has_side_effects=True),
+        compiler_params=pltpu.CompilerParams(collective_id=1, has_side_effects=True, vmem_limit_bytes=8 * 1024 * 1024),
         name="rim_exchange",
     )(low, high, sides)
-    density, charge = pl.pallas_call(
-        brick_kernel,
-        out_shape=(
-            jax.ShapeDtypeStruct(density.shape, BF16),
-            jax.ShapeDtypeStruct((BZ, BXY, BXY), F32),
-        ),
-        in_specs=[smem, smem, vmem, vmem, vmem, vmem, vmem, vmem, hbm],
-        out_specs=(hbm, hbm),
-        scratch_shapes=[tiles, pltpu.VMEM((2, BZ + 1, ROWS, 128), F32), dma((3,))],
-        compiler_params=params(),
-        name="brick",
-    )(anchor, near, own, below, above, low, high, sides, density)
+    density, charge = finish(brick, low, high, sides, density)
     return (density[None, None], charge)
 
 

time: 96.1 us -> 68.9 us (0.72)
  Pallas kernels: 85.9 us -> 68.1 us
  local copies, waits for them, and re-layouts: 8.89 us -> 0 us
    pallas_call x4, Pallas kernels: 85.9 us -> 68.1 us  [the longest x1 47.1 us: product(): pl.pallas_call(product_kernel, out_shape=(pltpu.VMEM((NC // 4, BLK, BLK),...]
    unnamed x21 -> x0, local copies, waits for them, and re-layouts: 8.32 us -> none
where the time goes in v2:
time: 68.9 us; the launch traced here: 68.8 us
  Pallas kernels  68.1 us (99%)
    pallas_call x1, Pallas kernels, product(): pl.pallas_call(product_kernel, out_shape=(pltpu.VMEM((NC // 4, BLK, BLK),...  47.1 us
    pallas_call x1, Pallas kernels, place(): pl.pallas_call(place_kernel, out_shape=(pltpu.VMEM((3, BZ + 1, ROWS, 128)...  9.64 us
    pallas_call x1, Pallas kernels, local(): pl.pallas_call(exchange_kernel, out_shape=(*(jax.ShapeDtypeStruct((BZ, 16...  9.03 us
    pallas_call x1, Pallas kernels, finish(): pl.pallas_call(charge_kernel, out_shape=(jax.ShapeDtypeStruct(density.sha...  2.36 us

profile of v2, /device:TPU:1, one launch (start us, length us, event | category | flops | bytes accessed | tf_op | source)
XLA Modules:
  0.0 68.8 jit_solution(11141544648857031210)
XLA Ops:
  0.6 47.1 %product_and_cubes.1 = (bf16[4,128,128]{2,1,0:T(8,128)(2,1)S(1)}, bf16[8,2,16,128]{3,2,1,0:T(8,128)(2,1)S(1)}, bf16[8,16,128]{2,1,0:T(8,128)(2,1)S(1)}, bf16[8,1...) custom-call(bf16[256,128]{1,0:T(8,128)(2,1)} %bitcast.13, bf16[512,128]{1,0:T(8,128)(2,1)} %bitcast.12, s32[8,8,16]{2,1,0:T(8,128)} %bitcast.14, ...), custom_call_target="tpu_custom_call" | custom-call | tf_op jit(solution)/shard_map/product_and_cubes/pallas_call | solution.py:302
  47.7 9.6 %place.1 = (f32[3,17,288,128]{3,2,1,0:T(8,128)S(1)}, bf16[16,16,128]{2,1,0:T(8,128)(2,1)S(1)}, bf16[16,16,128]{2,1,0:T(8,128)(2,1)S(1)}, bf16[288,128]{1,0:T(8,128)(2,1)S(1)}) custom-call(s32[3,3,1,64]{3,2,1,0:T(1,128)S(1)} %get-tuple-element.16.corner_ref, bf16[8,2,16,128]{3,2,1,0:T(8,128)(2,1)S(1)} %get-tuple-element.17.own_ref, ...), custom_call_target="tpu_custom_call" | custom-call | tf_op jit(solution)/shard_map/place/pallas_call | solution.py:508
  57.4 9.0 %rim_exchange.1 = (bf16[16,16,128]{2,1,0:T(8,128)(2,1)S(1)}, bf16[16,16,128]{2,1,0:T(8,128)(2,1)S(1)}, f32[256,128]{1,0:T(8,128)S(1)}) custom-call(bf16[16,16,128]{2,1,0:T(8,128)(2,1)S(1)} %get-tuple-element.21.low_ref, bf16[16,16,128]{2,1,0:T(8,128)(2,1)S(1)} %get-tuple-element.22.high_ref, bf16[288,128]{1,0:T(8,128)(2,1)S(1)} %get-tuple-element.23.sides_ref), custom_call_target="tpu_custom_call" | custom-call | tf_op jit(solution)/shard_map/rim_exchange/pallas_call | solution.py:553
  66.4 2.4 %charge.1 = (bf16[4,128,128]{2,1,0:T(8,128)(2,1)}, f32[16,256,256]{2,1,0:T(8,128)}) custom-call(f32[3,17,288,128]{3,2,1,0:T(8,128)S(1)} %get-tuple-element.20.brick, bf16[16,16,128]{2,1,0:T(8,128)(2,1)S(1)} %get-tuple-element.24.low_ref, bf16[16,16,128]{2,1,0:T(8,128)(2,1)S(1)} %get-tuple-element.25.high_ref, f32[256,128]{1,0:T(8,128)S(1)} %get-tuple-element.26.sides_ref, ...), custom_call_target="tpu_custom_call" | custom-call | tf_op jit(solution)/shard_map/charge/pallas_call | solution.py:522

commit v3 on v2

--- a/solution.py
+++ b/solution.py
@@ -376,67 +376,65 @@
             for q in range(2):
                 for r in range(8):
                     for w in range(2):
-                        tiles[i, q * 2 + w, r * 8 + s] = out[(q * 8 + r) * 8 : (q * 8 + r) * 8 + 8, w * 128 : w * 128 + 128]
-
-
-def place_kernel(corner_ref, own_ref, below_ref, above_ref, brick, low_ref, high_ref, sides_ref, tiles, sides):
+                        tiles[i * 4 + q * 2 + w, r * 8 + s] = out[(q * 8 + r) * 8 : (q * 8 + r) * 8 + 8, w * 128 : w * 128 + 128]
+
+
+def place_kernel(corner_ref, own_ref, below_ref, above_ref, brick, low_ref, high_ref, sides_ref, ends_ref, tiles, sides):
     anchor_ref, near_ref = corner_ref.at[0], corner_ref.at[pl.ds(1, 2)]
     for h in range(2):
 
         @pl.loop(0, BZ)
         def _(z):
-            brick[h, z, 8 : 24 + BXY, :] = jnp.zeros((16 + BXY, 128), F32)
+            brick[h, z + HALO, 8 : 24 + BXY, :] = jnp.zeros((16 + BXY, 128), F32)
 
     sides[...] = jnp.zeros_like(sides)
     spread_tiles(anchor_ref, near_ref, own_ref, below_ref, above_ref, tiles)
     lane = lax.broadcasted_iota(jnp.int32, (8, 128), 1)
 
-    def add(parts, k, oz, ox, oy):
+    def add(half, count, shift, k, oz, ox, oy):
         first = jnp.maximum(oy - HALO, 0) // 128
         rows = pl.ds(ox + 16 - HALO, 8)
+        planes = pl.ds(oz + shift, count)
         for h in (first, first + 1):
             t = lane + (h * 128 - oy + HALO)
             inside = (t >= 0) & (t < 8)
-            at = []
-            for _, _, dz in parts:
-                z = oz + dz
-                at.append((h, jnp.where((z >= 0) & (z < BZ), z, BZ), rows))
-            new = [brick[x] + jnp.where(inside, tiles[i, w, k], 0.0) for x, (i, w, _) in zip(at, parts)]
-            for x, v in zip(at, new):
-                brick[x] = v
+            brick[h, planes, rows, :] += jnp.where(inside[None], tiles[4 * half : 4 * half + count, k], 0.0)
 
         @pl.when((oy < HALO) | (oy > BXY - HALO))
         def _():
-            for i, w, dz in parts:
-                z = oz + dz
+            for w in range(count):
+                z = oz + shift + w - HALO
                 start = jnp.where(oy < HALO, z * 4, 64 + z * 4)
                 base = start + jnp.where(oy < HALO, oy, oy - (BXY + HALO))
-                u = pltpu.roll(tiles[i, w, k], lax.rem(base - oy + HALO + 512, 8), 1)
+                u = pltpu.roll(tiles[4 * half + w, k], lax.rem(base - oy + HALO + 512, 8), 1)
                 t = lane - base
                 inside = (t >= 0) & (t < 8) & (lane >= start) & (lane < start + 4) & (z >= 0) & (z < BZ)
                 sides[rows, :] += jnp.where(inside, u, 0.0)
 
-    @pl.loop(0, anchor_ref.shape[2])
+    @pl.loop(0, corner_ref.shape[3])
     def _(k):
-        add([(a // 4, a % 4, a - 4) for a in range(8)], k, anchor_ref[0, 0, k], anchor_ref[1, 0, k], anchor_ref[2, 0, k])
-
-    @pl.loop(0, anchor_ref.shape[2])
-    def _(k):
+        add(0, 8, 0, k, anchor_ref[0, 0, k], anchor_ref[1, 0, k], anchor_ref[2, 0, k])
+
         @pl.when(near_ref[0, 0, 0, k] > BZ - HALO)
         def _():
-            add([(2, w, w - BZ) for w in range(4)], k, near_ref[0, 0, 0, k], near_ref[0, 1, 0, k], near_ref[0, 2, 0, k])
+            add(2, 4, HALO - BZ, k, near_ref[0, 0, 0, k], near_ref[0, 1, 0, k], near_ref[0, 2, 0, k])
 
         @pl.when(near_ref[1, 0, 0, k] < HALO)
         def _():
-            add([(3, w, w - HALO + BZ) for w in range(4)], k, near_ref[1, 0, 0, k], near_ref[1, 1, 0, k], near_ref[1, 2, 0, k])
+            add(3, 4, BZ, k, near_ref[1, 0, 0, k], near_ref[1, 1, 0, k], near_ref[1, 2, 0, k])
 
     for z in range(BZ):
-        low_ref[z] = jnp.concatenate([brick[h, z, 8:16] for h in range(2)], axis=0).astype(BF16)
-        high_ref[z] = jnp.concatenate([brick[h, z, 16 + BXY : 24 + BXY] for h in range(2)], axis=0).astype(BF16)
-    sides_ref[...] = sides[...].astype(BF16)
-
-
-def exchange_kernel(low_ref, high_ref, sides_ref, low_out, high_out, sides_out, low_in, high_in, sides_in, send_sem, recv_sem):
+        low_ref[z] = jnp.concatenate([brick[h, z + HALO, 8:16] for h in range(2)], axis=0).astype(BF16)
+        high_ref[z] = jnp.concatenate([brick[h, z + HALO, 16 + BXY : 24 + BXY] for h in range(2)], axis=0).astype(BF16)
+    one, two = sides[16 : 16 + BXY // 2, :], sides[16 + BXY // 2 : 16 + BXY, :]
+    left = lax.broadcasted_iota(jnp.int32, one.shape, 1) < 64
+    sides_ref[0] = jnp.where(left, one, pltpu.roll(two, 64, 1)).astype(BF16)
+    sides_ref[1] = jnp.where(left, pltpu.roll(one, 64, 1), two).astype(BF16)
+    ends_ref[0] = sides[0:16, :].astype(BF16)
+    ends_ref[1] = sides[16 + BXY : 32 + BXY, :].astype(BF16)
+
+
+def exchange_kernel(low_ref, high_ref, sides_ref, ends_ref, low_out, high_out, sides_out, low_in, high_in, sides_in, ends_in, send_sem, recv_sem):
     nr, nc = lax.axis_size("row"), lax.axis_size("col")
     r, c, d = lax.axis_index("row"), lax.axis_index("col"), lax.axis_index("depth")
     barrier = pltpu.get_barrier_semaphore()
@@ -446,16 +444,15 @@
                 to = (lax.rem(r + i, nr), lax.rem(c + j, nc), d)
                 pl.semaphore_signal(barrier, inc=1, device_id=to, device_id_type=MESH)
     pl.semaphore_wait(barrier, 8)
-    first, middle, last = pl.ds(0, 16), pl.ds(16, BXY), pl.ds(16 + BXY, 16)
     plan = [
-        (0, nc - 1, sides_ref.at[middle], sides_in.at[1, middle]),
-        (0, 1, sides_ref.at[middle], sides_in.at[0, middle]),
+        (0, nc - 1, sides_ref.at[0], sides_in.at[0]),
+        (0, 1, sides_ref.at[1], sides_in.at[1]),
         (nr - 1, 0, low_ref, low_in),
         (1, 0, high_ref, high_in),
-        (nr - 1, nc - 1, sides_ref.at[first], sides_in.at[1, last]),
-        (nr - 1, 1, sides_ref.at[first], sides_in.at[0, last]),
-        (1, nc - 1, sides_ref.at[last], sides_in.at[1, first]),
-        (1, 1, sides_ref.at[last], sides_in.at[0, first]),
+        (nr - 1, nc - 1, ends_ref.at[0], ends_in.at[0]),
+        (nr - 1, 1, ends_ref.at[0], ends_in.at[1]),
+        (1, nc - 1, ends_ref.at[1], ends_in.at[2]),
+        (1, 1, ends_ref.at[1], ends_in.at[3]),
     ]
     copies = []
     for n, (i, j, src, dst) in enumerate(plan):
@@ -469,14 +466,15 @@
         copy.wait()
     low_out[...] = low_in[...]
     high_out[...] = high_in[...]
-    lane = lax.broadcasted_iota(jnp.int32, (BXY, 128), 1)
-    sides = jnp.where(lane < 64, sides_in[1, middle, :].astype(F32), sides_in[0, middle, :].astype(F32))
-    sides_out[...] = sides
-    for at, rows in ((first, pl.ds(0, 8)), (last, pl.ds(BXY - 8, 8))):
-        got = jnp.where(
-            lax.broadcasted_iota(jnp.int32, (16, 128), 1) < 64, sides_in[1, at, :].astype(F32), sides_in[0, at, :].astype(F32)
-        )
-        sides_out[rows, :] += got[0:8] if at is first else got[8:16]
+    right, left = sides_in[0].astype(F32), sides_in[1].astype(F32)
+    lower = lax.broadcasted_iota(jnp.int32, right.shape, 1) < 64
+    sides_out[0 : BXY // 2, :] = jnp.where(lower, right, pltpu.roll(left, 64, 1))
+    sides_out[BXY // 2 : BXY, :] = jnp.where(lower, pltpu.roll(right, 64, 1), left)
+    lower = lax.broadcasted_iota(jnp.int32, (16, 128), 1) < 64
+    after = jnp.where(lower, ends_in[0].astype(F32), ends_in[1].astype(F32))
+    before = jnp.where(lower, ends_in[2].astype(F32), ends_in[3].astype(F32))
+    sides_out[0:8, :] += before[0:8]
+    sides_out[BXY - 8 : BXY, :] += after[8:16]
 
 
 def charge_kernel(brick, low_ref, high_ref, sides_ref, density_ref, density_out, charge_ref, full, sems):
@@ -491,7 +489,7 @@
         out = jnp.dot(sides, unfold, preferred_element_type=F32)
         for h in range(2):
             lanes = slice(h * 128, h * 128 + 128)
-            full[z, :, lanes] = out[:, lanes] + brick[h, z, 16 : 16 + BXY, :]
+            full[z, :, lanes] = out[:, lanes] + brick[h, z + HALO, 16 : 16 + BXY, :]
             full[z, 0:8, lanes] += high_ref[z].astype(F32)[8 * h : 8 * h + 8]
             full[z, BXY - 8 : BXY, lanes] += low_ref[z].astype(F32)[8 * h : 8 * h + 8]
         copies.append(pltpu.make_async_copy(full.at[z], charge_ref.at[z], sems.at[z]))
@@ -507,11 +505,11 @@
     faces = (jax.ShapeDtypeStruct((BZ, 16, 128), BF16),) * 2
     return pl.pallas_call(
         place_kernel,
-        out_shape=(pltpu.VMEM((3, BZ + 1, ROWS, 128), F32), *faces, jax.ShapeDtypeStruct((ROWS, 128), BF16)),
+        out_shape=(pltpu.VMEM((3, BZ + 2 * HALO, ROWS, 128), F32), *faces, jax.ShapeDtypeStruct((2, BXY // 2, 128), BF16), jax.ShapeDtypeStruct((2, 16, 128), BF16)),
         in_specs=[smem, vmem, vmem, vmem],
-        out_specs=(vmem, vmem, vmem, vmem),
-        scratch_shapes=[pltpu.VMEM((4, 4, nk, 8, 128), F32), pltpu.VMEM((ROWS, 128), F32)],
-        compiler_params=pltpu.CompilerParams(vmem_limit_bytes=24 * 1024 * 1024),
+        out_specs=(vmem,) * 5,
+        scratch_shapes=[pltpu.VMEM((16, nk, 8, 128), F32), pltpu.VMEM((ROWS, 128), F32)],
+        compiler_params=pltpu.CompilerParams(vmem_limit_bytes=32 * 1024 * 1024),
         name="place",
     )(corner, own, below, above)
 
@@ -528,7 +526,7 @@
         in_specs=[vmem, vmem, vmem, vmem, vmem],
         out_specs=(hbm, hbm),
         scratch_shapes=[pltpu.VMEM((BZ, BXY, BXY), F32), pltpu.SemaphoreType.DMA((BZ + 1,))],
-        compiler_params=pltpu.CompilerParams(vmem_limit_bytes=24 * 1024 * 1024),
+        compiler_params=pltpu.CompilerParams(vmem_limit_bytes=32 * 1024 * 1024),
         name="charge",
     )(brick, low, high, sides, density)
 
@@ -549,22 +547,23 @@
     )
     vmem = pl.BlockSpec(memory_space=pltpu.VMEM)
     dma = pltpu.SemaphoreType.DMA
-    brick, low, high, sides = place(corner, own, below, above)
+    brick, low, high, sides, ends = place(corner, own, below, above)
     low, high, sides = pl.pallas_call(
         exchange_kernel,
         out_shape=(*(jax.ShapeDtypeStruct((BZ, 16, 128), BF16),) * 2, jax.ShapeDtypeStruct((BXY, 128), F32)),
-        in_specs=[vmem, vmem, vmem],
+        in_specs=[vmem, vmem, vmem, vmem],
         out_specs=(vmem, vmem, vmem),
         scratch_shapes=[
             pltpu.VMEM((BZ, 16, 128), BF16),
             pltpu.VMEM((BZ, 16, 128), BF16),
-            pltpu.VMEM((2, ROWS, 128), BF16),
+            pltpu.VMEM((2, BXY // 2, 128), BF16),
+            pltpu.VMEM((4, 16, 128), BF16),
             dma((8,)),
             dma((8,)),
         ],
         compiler_params=pltpu.CompilerParams(collective_id=1, has_side_effects=True, vmem_limit_bytes=8 * 1024 * 1024),
         name="rim_exchange",
-    )(low, high, sides)
+    )(low, high, sides, ends)
     density, charge = finish(brick, low, high, sides, density)
     return (density[None, None], charge)
 

time: 68.9 us -> 66.7 us (0.968)
  Pallas kernels: 68.1 us -> 66 us
    pallas_call x1, Pallas kernels: 9.64 us -> 8.15 us  [place(): pl.pallas_call(place_kernel, out_shape=(pltpu.VMEM((3, BZ + 2 * HALO, ROW...]
where the time goes in v3:
time: 66.7 us; the launch traced here: 66.6 us
  Pallas kernels  66 us (99%)
    pallas_call x1, Pallas kernels, product(): pl.pallas_call(product_kernel, out_shape=(pltpu.VMEM((NC // 4, BLK, BLK),...  47.1 us
    pallas_call x1, Pallas kernels, local(): pl.pallas_call(exchange_kernel, out_shape=(*(jax.ShapeDtypeStruct((BZ, 16...  8.34 us
    pallas_call x1, Pallas kernels, place(): pl.pallas_call(place_kernel, out_shape=(pltpu.VMEM((3, BZ + 2 * HALO, ROW...  8.15 us
    pallas_call x1, Pallas kernels, finish(): pl.pallas_call(charge_kernel, out_shape=(jax.ShapeDtypeStruct(density.sha...  2.36 us

profile of v3, /device:TPU:1, one launch (start us, length us, event | category | flops | bytes accessed | tf_op | source)
XLA Modules:
  0.0 66.6 jit_solution(12157657236838686350)
XLA Ops:
  0.6 47.1 %product_and_cubes.1 = (bf16[4,128,128]{2,1,0:T(8,128)(2,1)S(1)}, bf16[8,2,16,128]{3,2,1,0:T(8,128)(2,1)S(1)}, bf16[8,16,128]{2,1,0:T(8,128)(2,1)S(1)}, bf16[8,1...) custom-call(bf16[256,128]{1,0:T(8,128)(2,1)} %bitcast.13, bf16[512,128]{1,0:T(8,128)(2,1)} %bitcast.12, s32[8,8,16]{2,1,0:T(8,128)} %bitcast.14, ...), custom_call_target="tpu_custom_call" | custom-call | tf_op jit(solution)/shard_map/product_and_cubes/pallas_call | solution.py:302
  47.7 8.1 %place.1 = (f32[3,24,288,128]{3,2,1,0:T(8,128)S(1)}, bf16[16,16,128]{2,1,0:T(8,128)(2,1)S(1)}, bf16[16,16,128]{2,1,0:T(8,128)(2,1)S(1)}, bf16[2,128,128]{2,1,0:T(8,128)(2,1)S(1)}, bf16[2,16,128]{2,1,0:T(8,128)(2,1)S(1)}) custom-call(s32[3,3,1,64]{3,2,1,0:T(1,128)S(1)} %get-tuple-element.17.corner_ref, bf16[8,2,16,128]{3,2,1,0:T(8,128)(2,1)S(1)} %get-tuple-element.18.own_ref, ...), custom_call_target="tpu_custom_call" | custom-call | tf_op jit(solution)/shard_map/place/pallas_call | solution.py:506
  55.9 8.3 %rim_exchange.1 = (bf16[16,16,128]{2,1,0:T(8,128)(2,1)S(1)}, bf16[16,16,128]{2,1,0:T(8,128)(2,1)S(1)}, f32[256,128]{1,0:T(8,128)S(1)}) custom-call(bf16[16,16,128]{2,1,0:T(8,128)(2,1)S(1)} %get-tuple-element.22.low_ref, bf16[16,16,128]{2,1,0:T(8,128)(2,1)S(1)} %get-tuple-element.23.high_ref, bf16[2,128,128]{2,1,0:T(8,128)(2,1)S(1)} %get-tuple-element.24.sides_ref, ...), custom_call_target="tpu_custom_call" | custom-call | tf_op jit(solution)/shard_map/rim_exchange/pallas_call | solution.py:551
  64.2 2.4 %charge.1 = (bf16[4,128,128]{2,1,0:T(8,128)(2,1)}, f32[16,256,256]{2,1,0:T(8,128)}) custom-call(f32[3,24,288,128]{3,2,1,0:T(8,128)S(1)} %get-tuple-element.21.brick, bf16[16,16,128]{2,1,0:T(8,128)(2,1)S(1)} %get-tuple-element.26.low_ref, bf16[16,16,128]{2,1,0:T(8,128)(2,1)S(1)} %get-tuple-element.27.high_ref, f32[256,128]{1,0:T(8,128)S(1)} %get-tuple-element.28.sides_ref, ...), custom_call_target="tpu_custom_call" | custom-call | tf_op jit(solution)/shard_map/charge/pallas_call | solution.py:520

commit v4 on v3

--- a/solution.py
+++ b/solution.py
@@ -360,7 +360,7 @@
             y = jnp.where(lax.rem(row16, 8) == r, corner(r * 8 + s) - HALO, y)
         return lane16 - lax.rem(lane16, 8) + lax.rem(lane16 - y + BXY * 2, 8)
 
-    @pl.loop(0, own_ref.shape[0])
+    @pl.loop(0, own_ref.shape[0], unroll=8)
     def _(s):
         index = turn(lambda k: anchor_ref[2, 0, k], s)
         parts = [(own_ref[s, 0], index), (own_ref[s, 1], index)]
@@ -380,7 +380,6 @@
 
 
 def place_kernel(corner_ref, own_ref, below_ref, above_ref, brick, low_ref, high_ref, sides_ref, ends_ref, tiles, sides):
-    anchor_ref, near_ref = corner_ref.at[0], corner_ref.at[pl.ds(1, 2)]
     for h in range(2):
 
         @pl.loop(0, BZ)
@@ -388,40 +387,62 @@
             brick[h, z + HALO, 8 : 24 + BXY, :] = jnp.zeros((16 + BXY, 128), F32)
 
     sides[...] = jnp.zeros_like(sides)
-    spread_tiles(anchor_ref, near_ref, own_ref, below_ref, above_ref, tiles)
+    spread_tiles(corner_ref.at[0], corner_ref.at[pl.ds(1, 2)], own_ref, below_ref, above_ref, tiles)
     lane = lax.broadcasted_iota(jnp.int32, (8, 128), 1)
 
-    def add(half, count, shift, k, oz, ox, oy):
+    def add(half, count, start, k, ox, oy):
         first = jnp.maximum(oy - HALO, 0) // 128
         rows = pl.ds(ox + 16 - HALO, 8)
-        planes = pl.ds(oz + shift, count)
+        planes = pl.ds(start, count)
         for h in (first, first + 1):
             t = lane + (h * 128 - oy + HALO)
             inside = (t >= 0) & (t < 8)
             brick[h, planes, rows, :] += jnp.where(inside[None], tiles[4 * half : 4 * half + count, k], 0.0)
 
-        @pl.when((oy < HALO) | (oy > BXY - HALO))
+    def add_rim(half, count, shift, k, oz, ox, oy):
+        for w in range(count):
+            z = oz + shift + w - HALO
+            start = jnp.where(oy < HALO, z * 4, 64 + z * 4)
+            base = start + jnp.where(oy < HALO, oy, oy - (BXY + HALO))
+            u = pltpu.roll(tiles[4 * half + w, k], lax.rem(base - oy + HALO + 512, 8), 1)
+            t = lane - base
+            inside = (t >= 0) & (t < 8) & (lane >= start) & (lane < start + 4) & (z >= 0) & (z < BZ)
+            sides[pl.ds(ox + 16 - HALO, 8), :] += jnp.where(inside, u, 0.0)
+
+    def corner(i, k):
+        return corner_ref[i, 0, 0, k], corner_ref[i, 1, 0, k], corner_ref[i, 2, 0, k]
+
+    def is_rim(oy):
+        return (oy < HALO) | (oy > BXY - HALO)
+
+    nk = corner_ref.shape[3]
+
+    @pl.loop(0, nk, unroll=4)
+    def _(k):
+        z, x, y = corner(0, k)
+        add(0, 8, z, k, x, y)
+        z, x, y = corner(1, k)
+        add(2, 4, jnp.where(z > BZ - HALO, z + HALO - BZ, BZ + HALO), k, x, y)
+        z, x, y = corner(2, k)
+        add(3, 4, jnp.where(z < HALO, z + BZ, BZ + HALO), k, x, y)
+
+    @pl.loop(0, nk)
+    def _(k):
+        y0, y1, y2 = corner_ref[0, 2, 0, k], corner_ref[1, 2, 0, k], corner_ref[2, 2, 0, k]
+
+        @pl.when(is_rim(y0) | is_rim(y1) | is_rim(y2))
         def _():
-            for w in range(count):
-                z = oz + shift + w - HALO
-                start = jnp.where(oy < HALO, z * 4, 64 + z * 4)
-                base = start + jnp.where(oy < HALO, oy, oy - (BXY + HALO))
-                u = pltpu.roll(tiles[4 * half + w, k], lax.rem(base - oy + HALO + 512, 8), 1)
-                t = lane - base
-                inside = (t >= 0) & (t < 8) & (lane >= start) & (lane < start + 4) & (z >= 0) & (z < BZ)
-                sides[rows, :] += jnp.where(inside, u, 0.0)
-
-    @pl.loop(0, corner_ref.shape[3])
-    def _(k):
-        add(0, 8, 0, k, anchor_ref[0, 0, k], anchor_ref[1, 0, k], anchor_ref[2, 0, k])
-
-        @pl.when(near_ref[0, 0, 0, k] > BZ - HALO)
-        def _():
-            add(2, 4, HALO - BZ, k, near_ref[0, 0, 0, k], near_ref[0, 1, 0, k], near_ref[0, 2, 0, k])
-
-        @pl.when(near_ref[1, 0, 0, k] < HALO)
-        def _():
-            add(3, 4, BZ, k, near_ref[1, 0, 0, k], near_ref[1, 1, 0, k], near_ref[1, 2, 0, k])
+            @pl.when(is_rim(y0))
+            def _():
+                add_rim(0, 8, 0, k, *corner(0, k))
+
+            @pl.when(is_rim(y1))
+            def _():
+                add_rim(2, 4, HALO - BZ, k, *corner(1, k))
+
+            @pl.when(is_rim(y2))
+            def _():
+                add_rim(3, 4, BZ, k, *corner(2, k))
 
     for z in range(BZ):
         low_ref[z] = jnp.concatenate([brick[h, z + HALO, 8:16] for h in range(2)], axis=0).astype(BF16)

time: 66.7 us -> 64.7 us (0.970)
  Pallas kernels: 66 us -> 63.9 us
    pallas_call x1, Pallas kernels: 8.15 us -> 6.25 us  [place(): pl.pallas_call(place_kernel, out_shape=(pltpu.VMEM((3, BZ + 2 * HALO, ROW...]
where the time goes in v4:
time: 64.7 us; the launch traced here: 64.6 us
  Pallas kernels  63.9 us (99%)
  between operations  0.65 us (1%)
    pallas_call x1, Pallas kernels, product(): pl.pallas_call(product_kernel, out_shape=(pltpu.VMEM((NC // 4, BLK, BLK),...  47.1 us
    pallas_call x1, Pallas kernels, local(): pl.pallas_call(exchange_kernel, out_shape=(*(jax.ShapeDtypeStruct((BZ, 16...  8.19 us
    pallas_call x1, Pallas kernels, place(): pl.pallas_call(place_kernel, out_shape=(pltpu.VMEM((3, BZ + 2 * HALO, ROW...  6.25 us
    pallas_call x1, Pallas kernels, finish(): pl.pallas_call(charge_kernel, out_shape=(jax.ShapeDtypeStruct(density.sha...  2.36 us

profile of v4, /device:TPU:1, one launch (start us, length us, event | category | flops | bytes accessed | tf_op | source)
XLA Modules:
  0.0 64.6 jit_solution(2770882002749846524)
XLA Ops:
  0.6 47.1 %product_and_cubes.1 = (bf16[4,128,128]{2,1,0:T(8,128)(2,1)S(1)}, bf16[8,2,16,128]{3,2,1,0:T(8,128)(2,1)S(1)}, bf16[8,16,128]{2,1,0:T(8,128)(2,1)S(1)}, bf16[8,1...) custom-call(bf16[256,128]{1,0:T(8,128)(2,1)} %bitcast.13, bf16[512,128]{1,0:T(8,128)(2,1)} %bitcast.12, s32[8,8,16]{2,1,0:T(8,128)} %bitcast.14, ...), custom_call_target="tpu_custom_call" | custom-call | tf_op jit(solution)/shard_map/product_and_cubes/pallas_call | solution.py:302
  47.7 6.2 %place.1 = (f32[3,24,288,128]{3,2,1,0:T(8,128)S(1)}, bf16[16,16,128]{2,1,0:T(8,128)(2,1)S(1)}, bf16[16,16,128]{2,1,0:T(8,128)(2,1)S(1)}, bf16[2,128,128]{2,1,0:T(8,128)(2,1)S(1)}, bf16[2,16,128]{2,1,0:T(8,128)(2,1)S(1)}) custom-call(s32[3,3,1,64]{3,2,1,0:T(1,128)S(1)} %get-tuple-element.17.corner_ref, bf16[8,2,16,128]{3,2,1,0:T(8,128)(2,1)S(1)} %get-tuple-element.18.own_ref, ...), custom_call_target="tpu_custom_call" | custom-call | tf_op jit(solution)/shard_map/place/pallas_call | solution.py:527
  54.0 8.2 %rim_exchange.1 = (bf16[16,16,128]{2,1,0:T(8,128)(2,1)S(1)}, bf16[16,16,128]{2,1,0:T(8,128)(2,1)S(1)}, f32[256,128]{1,0:T(8,128)S(1)}) custom-call(bf16[16,16,128]{2,1,0:T(8,128)(2,1)S(1)} %get-tuple-element.22.low_ref, bf16[16,16,128]{2,1,0:T(8,128)(2,1)S(1)} %get-tuple-element.23.high_ref, bf16[2,128,128]{2,1,0:T(8,128)(2,1)S(1)} %get-tuple-element.24.sides_ref, ...), custom_call_target="tpu_custom_call" | custom-call | tf_op jit(solution)/shard_map/rim_exchange/pallas_call | solution.py:572
  62.2 2.4 %charge.1 = (bf16[4,128,128]{2,1,0:T(8,128)(2,1)}, f32[16,256,256]{2,1,0:T(8,128)}) custom-call(f32[3,24,288,128]{3,2,1,0:T(8,128)S(1)} %get-tuple-element.21.brick, bf16[16,16,128]{2,1,0:T(8,128)(2,1)S(1)} %get-tuple-element.26.low_ref, bf16[16,16,128]{2,1,0:T(8,128)(2,1)S(1)} %get-tuple-element.27.high_ref, f32[256,128]{1,0:T(8,128)S(1)} %get-tuple-element.28.sides_ref, ...), custom_call_target="tpu_custom_call" | custom-call | tf_op jit(solution)/shard_map/charge/pallas_call | solution.py:541

commit v5 on v4

--- a/solution.py
+++ b/solution.py
@@ -70,19 +70,19 @@
     pl.semaphore_wait(barrier, greeted)
 
     copies = []
-    right, left = up(c, 1, nc), up(c, nc - 1, nc)
     chip_r, chip_l = up(chip, 1, chips) * 2 + core, up(chip, chips - 1, chips) * 2 + core
     half = nc // 2
 
     def x_step(h):
+        hop = min(h, 2)
         rows_r = pl.ds(0, 256) if h < half else pl.ds(0, 128)
         rows_l = pl.ds(0, 256) if h < half else pl.ds(128, 128)
-        src_r, src_l = up(c, nc - (h - 1), nc), up(c, h - 1, nc)
+        src_r, src_l = up(c, nc - (h - hop), nc), up(c, h - hop, nc)
         copies.append(
-            send((x_ref if h == 1 else xg.at[src_r]).at[rows_r], xg.at[src_r, rows_r], xr_send.at[h - 1], xr_recv.at[h - 1], r, right, d)
+            send((x_ref if h == hop else xg.at[src_r]).at[rows_r], xg.at[src_r, rows_r], xr_send.at[h - 1], xr_recv.at[h - 1], r, up(c, hop, nc), d)
         )
         copies.append(
-            send((x_ref if h == 1 else xg.at[src_l]).at[rows_l], xg.at[src_l, rows_l], xl_send.at[h - 1], xl_recv.at[h - 1], r, left, d)
+            send((x_ref if h == hop else xg.at[src_l]).at[rows_l], xg.at[src_l, rows_l], xl_send.at[h - 1], xl_recv.at[h - 1], r, up(c, nc - hop, nc), d)
         )
 
     def x_wait(h):
@@ -99,11 +99,13 @@
         slot = up(r, 2 * q, nr)
         copies.append(send(y_ref if q == 0 else yg.at[slot], yg.at[slot], ys_send.at[q], ys_recv.at[q], sibling, c, d))
 
-    whole, lower, upper = pl.ds(0, 512), pl.ds(0, 256), pl.ds(256, 256)
+    whole = pl.ds(0, 512)
     x_step(1)
-    y_share(0)
     copies.append(send(y_ref, yg.at[r], yr_send.at[0], yr_recv.at[0], chip_r, c, d))
     copies.append(send(y_ref, yg.at[r], yl_send.at[0], yl_recv.at[0], chip_l, c, d))
+    x_step(2)
+    copies.append(send(y_ref, yg.at[r], yr_send.at[1], yr_recv.at[1], up(r, 4, nr), c, d))
+    y_share(0)
     for i, k in enumerate((1, nd - 1)):
         copies.append(send(anchor_ref, near_anchor_ref.at[i], anchor_send.at[i], anchor_recv.at[i], r, c, up(d, k, nd)))
 
@@ -174,25 +176,19 @@
     panel(0)
     loads[4].wait()
     x_wait(1)
-    x_step(2)
+    x_step(3)
     y_wait(up(r, nr - 2, nr), whole, yr_recv.at[0])
-    copies.append(
-        send(yg.at[up(r, nr - 2, nr), lower], yg.at[up(r, nr - 2, nr), lower], yr_send.at[1], yr_recv.at[1], chip_r, c, d)
-    )
     y_wait(up(r, 2, nr), whole, yl_recv.at[0])
-    copies.append(send(yg.at[up(r, 2, nr), upper], yg.at[up(r, 2, nr), upper], yl_send.at[1], yl_recv.at[1], chip_l, c, d))
     y_share(chips - 1)
     y_share(1)
     basis(0, quarter)
     x_wait(2)
-    x_step(3)
-    y_wait(up(r, 4, nr), lower, yr_recv.at[1])
-    y_wait(up(r, 4, nr), upper, yl_recv.at[1])
+    x_step(4)
+    y_wait(up(r, 4, nr), whole, yr_recv.at[1])
     y_share(2)
     panel(2)
     panel(nr - 2)
     x_wait(3)
-    x_step(4)
     for q in range(chips):
         y_wait(lax.rem(sibling + 2 * q, nr), whole, ys_recv.at[q])
     for delta in (1, nr - 1, 3, nr - 3):
@@ -334,7 +330,7 @@
             pltpu.VMEM((nc, 16, 128), BF16),
             pltpu.VMEM((nc, 16, 128), BF16),
             dma((4,)), dma((4,)), dma((4,)), dma((4,)),
-            dma((2,)), dma((2,)), dma((2,)), dma((2,)), dma((4,)), dma((4,)),
+            dma((2,)), dma((2,)), dma((1,)), dma((1,)), dma((4,)), dma((4,)),
             dma((3,)), dma((3,)), dma((8,)), dma((8,)), dma((3, 8)), dma((3, 8)), dma((2,)), dma((2,)), dma((5,)),
         ],
         compiler_params=pltpu.CompilerParams(collective_id=0, has_side_effects=True, vmem_limit_bytes=56 * 1024 * 1024),

time: 64.7 us -> 63.8 us (0.986)
  Pallas kernels: 63.9 us -> 63 us
    pallas_call x1, Pallas kernels: 47.1 us -> 46.5 us  [product(): pl.pallas_call(product_kernel, out_shape=(pltpu.VMEM((NC // 4, BLK, BLK),...]
where the time goes in v5:
time: 63.8 us; the launch traced here: 63.7 us
  Pallas kernels  63 us (99%)
  between operations  0.65 us (1%)
    pallas_call x1, Pallas kernels, product(): pl.pallas_call(product_kernel, out_shape=(pltpu.VMEM((NC // 4, BLK, BLK),...  46.5 us
    pallas_call x1, Pallas kernels, local(): pl.pallas_call(exchange_kernel, out_shape=(*(jax.ShapeDtypeStruct((BZ, 16...  8.57 us
    pallas_call x1, Pallas kernels, place(): pl.pallas_call(place_kernel, out_shape=(pltpu.VMEM((3, BZ + 2 * HALO, ROW...  5.63 us
    pallas_call x1, Pallas kernels, finish(): pl.pallas_call(charge_kernel, out_shape=(jax.ShapeDtypeStruct(density.sha...  2.36 us

profile of v5, /device:TPU:1, one launch (start us, length us, event | category | flops | bytes accessed | tf_op | source)
XLA Modules:
  0.0 63.7 jit_solution(16960197702410584097)
XLA Ops:
  0.6 46.5 %product_and_cubes.1 = (bf16[4,128,128]{2,1,0:T(8,128)(2,1)S(1)}, bf16[8,2,16,128]{3,2,1,0:T(8,128)(2,1)S(1)}, bf16[8,16,128]{2,1,0:T(8,128)(2,1)S(1)}, bf16[8,1...) custom-call(bf16[256,128]{1,0:T(8,128)(2,1)} %bitcast.13, bf16[512,128]{1,0:T(8,128)(2,1)} %bitcast.12, s32[8,8,16]{2,1,0:T(8,128)} %bitcast.14, ...), custom_call_target="tpu_custom_call" | custom-call | tf_op jit(solution)/shard_map/product_and_cubes/pallas_call | solution.py:298
  47.1 5.6 %place.1 = (f32[3,24,288,128]{3,2,1,0:T(8,128)S(1)}, bf16[16,16,128]{2,1,0:T(8,128)(2,1)S(1)}, bf16[16,16,128]{2,1,0:T(8,128)(2,1)S(1)}, bf16[2,128,128]{2,1,0:T(8,128)(2,1)S(1)}, bf16[2,16,128]{2,1,0:T(8,128)(2,1)S(1)}) custom-call(s32[3,3,1,64]{3,2,1,0:T(1,128)S(1)} %get-tuple-element.17.corner_ref, bf16[8,2,16,128]{3,2,1,0:T(8,128)(2,1)S(1)} %get-tuple-element.18.own_ref, ...), custom_call_target="tpu_custom_call" | custom-call | tf_op jit(solution)/shard_map/place/pallas_call | solution.py:523
  52.7 8.6 %rim_exchange.1 = (bf16[16,16,128]{2,1,0:T(8,128)(2,1)S(1)}, bf16[16,16,128]{2,1,0:T(8,128)(2,1)S(1)}, f32[256,128]{1,0:T(8,128)S(1)}) custom-call(bf16[16,16,128]{2,1,0:T(8,128)(2,1)S(1)} %get-tuple-element.22.low_ref, bf16[16,16,128]{2,1,0:T(8,128)(2,1)S(1)} %get-tuple-element.23.high_ref, bf16[2,128,128]{2,1,0:T(8,128)(2,1)S(1)} %get-tuple-element.24.sides_ref, ...), custom_call_target="tpu_custom_call" | custom-call | tf_op jit(solution)/shard_map/rim_exchange/pallas_call | solution.py:568
  61.3 2.4 %charge.1 = (bf16[4,128,128]{2,1,0:T(8,128)(2,1)}, f32[16,256,256]{2,1,0:T(8,128)}) custom-call(f32[3,24,288,128]{3,2,1,0:T(8,128)S(1)} %get-tuple-element.21.brick, bf16[16,16,128]{2,1,0:T(8,128)(2,1)S(1)} %get-tuple-element.26.low_ref, bf16[16,16,128]{2,1,0:T(8,128)(2,1)S(1)} %get-tuple-element.27.high_ref, f32[256,128]{1,0:T(8,128)S(1)} %get-tuple-element.28.sides_ref, ...), custom_call_target="tpu_custom_call" | custom-call | tf_op jit(solution)/shard_map/charge/pallas_call | solution.py:537

commit v6 on v5

--- a/solution.py
+++ b/solution.py
@@ -188,11 +188,14 @@
     y_share(2)
     panel(2)
     panel(nr - 2)
+    for q in (0, 1, chips - 1):
+        y_wait(lax.rem(sibling + 2 * q, nr), whole, ys_recv.at[q])
+    panel(1)
+    panel(nr - 1)
     x_wait(3)
-    for q in range(chips):
-        y_wait(lax.rem(sibling + 2 * q, nr), whole, ys_recv.at[q])
-    for delta in (1, nr - 1, 3, nr - 3):
-        panel(delta)
+    y_wait(lax.rem(sibling + 4, nr), whole, ys_recv.at[2])
+    panel(3)
+    panel(nr - 3)
     x_wait(4)
     stage_panel(half)
     k = lax.rem(r + c + half, npanel)
@@ -265,7 +268,7 @@
         got = [first_in[q, pl.ds(s, 8, stride=8), :] for q in range(4)]
         for h in range(2):
             second_out[s, h] = jnp.concatenate(got[2 * h : 2 * h + 2], axis=0).astype(BF16)
-    for j in [*range(1, nc), 0]:
+    for j in (4, 3, 5, 2, 6, 1, 7, 0):
         s = up(c, j, nc)
         copies.append(send(second_out.at[s, 1], below_in.at[c], second_send.at[1, j], second_recv.at[1, c], r, s, up(d, 1, nd)))
         copies.append(send(second_out.at[s, 0], above_in.at[c], second_send.at[2, j], second_recv.at[2, c], r, s, up(d, nd - 1, nd)))

time: 63.8 us -> 62.4 us (0.978)
  Pallas kernels: 63 us -> 61.5 us
    pallas_call x1, Pallas kernels: 46.5 us -> 45.4 us  [product(): pl.pallas_call(product_kernel, out_shape=(pltpu.VMEM((NC // 4, BLK, BLK),...]
where the time goes in v6:
time: 62.4 us; the launch traced here: 62.1 us
  Pallas kernels  61.5 us (99%)
  between operations  0.65 us (1%)
    pallas_call x1, Pallas kernels, product(): pl.pallas_call(product_kernel, out_shape=(pltpu.VMEM((NC // 4, BLK, BLK),...  45.4 us
    pallas_call x1, Pallas kernels, local(): pl.pallas_call(exchange_kernel, out_shape=(*(jax.ShapeDtypeStruct((BZ, 16...  8.03 us
    pallas_call x1, Pallas kernels, place(): pl.pallas_call(place_kernel, out_shape=(pltpu.VMEM((3, BZ + 2 * HALO, ROW...  5.73 us
    pallas_call x1, Pallas kernels, finish(): pl.pallas_call(charge_kernel, out_shape=(jax.ShapeDtypeStruct(density.sha...  2.36 us

profile of v6, /device:TPU:1, one launch (start us, length us, event | category | flops | bytes accessed | tf_op | source)
XLA Modules:
  0.0 62.1 jit_solution(2267746476681197135)
XLA Ops:
  0.6 45.4 %product_and_cubes.1 = (bf16[4,128,128]{2,1,0:T(8,128)(2,1)S(1)}, bf16[8,2,16,128]{3,2,1,0:T(8,128)(2,1)S(1)}, bf16[8,16,128]{2,1,0:T(8,128)(2,1)S(1)}, bf16[8,1...) custom-call(bf16[256,128]{1,0:T(8,128)(2,1)} %bitcast.13, bf16[512,128]{1,0:T(8,128)(2,1)} %bitcast.12, s32[8,8,16]{2,1,0:T(8,128)} %bitcast.14, ...), custom_call_target="tpu_custom_call" | custom-call | tf_op jit(solution)/shard_map/product_and_cubes/pallas_call | solution.py:301
  46.0 5.7 %place.1 = (f32[3,24,288,128]{3,2,1,0:T(8,128)S(1)}, bf16[16,16,128]{2,1,0:T(8,128)(2,1)S(1)}, bf16[16,16,128]{2,1,0:T(8,128)(2,1)S(1)}, bf16[2,128,128]{2,1,0:T(8,128)(2,1)S(1)}, bf16[2,16,128]{2,1,0:T(8,128)(2,1)S(1)}) custom-call(s32[3,3,1,64]{3,2,1,0:T(1,128)S(1)} %get-tuple-element.17.corner_ref, bf16[8,2,16,128]{3,2,1,0:T(8,128)(2,1)S(1)} %get-tuple-element.18.own_ref, ...), custom_call_target="tpu_custom_call" | custom-call | tf_op jit(solution)/shard_map/place/pallas_call | solution.py:526
  51.7 8.0 %rim_exchange.1 = (bf16[16,16,128]{2,1,0:T(8,128)(2,1)S(1)}, bf16[16,16,128]{2,1,0:T(8,128)(2,1)S(1)}, f32[256,128]{1,0:T(8,128)S(1)}) custom-call(bf16[16,16,128]{2,1,0:T(8,128)(2,1)S(1)} %get-tuple-element.22.low_ref, bf16[16,16,128]{2,1,0:T(8,128)(2,1)S(1)} %get-tuple-element.23.high_ref, bf16[2,128,128]{2,1,0:T(8,128)(2,1)S(1)} %get-tuple-element.24.sides_ref, ...), custom_call_target="tpu_custom_call" | custom-call | tf_op jit(solution)/shard_map/rim_exchange/pallas_call | solution.py:571
  59.8 2.4 %charge.1 = (bf16[4,128,128]{2,1,0:T(8,128)(2,1)}, f32[16,256,256]{2,1,0:T(8,128)}) custom-call(f32[3,24,288,128]{3,2,1,0:T(8,128)S(1)} %get-tuple-element.21.brick, bf16[16,16,128]{2,1,0:T(8,128)(2,1)S(1)} %get-tuple-element.26.low_ref, bf16[16,16,128]{2,1,0:T(8,128)(2,1)S(1)} %get-tuple-element.27.high_ref, f32[256,128]{1,0:T(8,128)S(1)} %get-tuple-element.28.sides_ref, ...), custom_call_target="tpu_custom_call" | custom-call | tf_op jit(solution)/shard_map/charge/pallas_call | solution.py:540
